TPU v7x, 256 devices: a whole 4x4x8 slice. The times are simulated.
256 devices in a mesh: dp: 2 (over core), tm: 8 (over x_lo, y), height: 16 (over z, x_hi).
Axes of the slice: x: 4 (x_hi: 2, x_lo: 2; x = x_hi * 2 + x_lo), y: 4, z: 8, core: 2. Of those that a mesh axis runs over, the one named last changes fastest.
Arguments:
- inputs: bfloat16 [2, 32, 32, 192, 128], P('dp', 'tm', 'height'), may hold values from -6 to 6
- gain_in: float32 [192], replicated, may hold values from 0.5 to 1.5
- conv_in: bfloat16 [3, 3, 3, 96, 192], replicated, may hold values from -0.078125 to 0.078125
- gain_mid: float32 [96], replicated, may hold values from 0.5 to 1.5
- conv_mid: bfloat16 [3, 3, 3, 96, 96], replicated, may hold values from -0.125 to 0.125
- conv_skip: bfloat16 [96, 192], replicated, may hold values from -0.4375 to 0.4375
- scored_grads: bfloat16 [2, 16, 32, 96, 128], P('dp', 'tm', 'height'), may hold values from -6 to 6
- scored_frames: int32 [2, 16], P('dp'), may hold values from 0 to 31, as said below
Outputs:
- grad_inputs: bfloat16 [2, 32, 32, 192, 128], P('dp', 'tm', 'height')
- grad_conv_in: float32 [3, 3, 3, 96, 192], replicated
- grad_conv_mid: float32 [3, 3, 3, 96, 96], replicated
- grad_conv_skip: float32 [96, 192], replicated
Inputs may be any that keep to these rules, and one draw needn't show every extreme that they name: `scored_frames`: each clip's 16 entries are distinct frame numbers and always include 0 and 31.
All inputs are finite; a program needn't handle non-finite values.
Results may differ from a plain program's by a relative error of at most 0.013.
Values may be sent and summed in bfloat16 or wider, within the bound.
A program may use at most 64 MiB of HBM per device.

v0:
```python
import math

import jax
import jax.numpy as jnp
from jax import lax
from jax.sharding import PartitionSpec as P


def from_behind(value, axis, steps):
    count = lax.axis_size(axis)
    leading, last = (max(0, -steps), min(count, count - steps))
    return lax.ppermute(value, axis, [(source, source + steps) for source in range(leading, last)])


def with_halo(cells, sides, width):
    for axis, dim in sides:
        count = lax.axis_size(axis)
        ends = count - 1
        head = lax.slice_in_dim(cells, 0, width, axis=dim)
        tail = lax.slice_in_dim(cells, cells.shape[dim] - width, cells.shape[dim], axis=dim)
        cells = jnp.concatenate(
            [
                lax.ppermute(tail, axis, [(i, (i + 1) % count) for i in range(ends)]),
                cells,
                lax.ppermute(head, axis, [((i + 1) % count, i) for i in range(ends)]),
            ],
            axis=dim,
        )
    return cells


def act_norm(field, gain):
    mean_sq = jnp.mean(field * field, axis=2, keepdims=True)
    return jax.nn.silu(field * lax.rsqrt(mean_sq + 1e-06) * gain[:, None])


def shifted_stack(padded, cols, offsets):
    return jnp.concatenate([padded[..., k : k + cols] for k in offsets], axis=2)


def taps_forward(padded, weight, frames, rows, cols):
    stack = shifted_stack(padded, cols, (0, 1, 2))
    out_ch = weight.shape[3]
    total = jnp.zeros((frames, rows, out_ch, cols), jnp.float32)
    for kt in range(3):
        for kh in range(3):
            matrix = weight[kt, kh].transpose(1, 0, 2).reshape(out_ch, -1)
            window = stack[kt : kt + frames, kh : kh + rows]
            total = total + jnp.einsum(
                "om,fhmw->fhow", matrix, window, preferred_element_type=jnp.float32
            )
    return total


def taps_input(padded, weight, frames, rows, cols):
    stack = shifted_stack(padded, cols, (2, 1, 0))
    in_ch = weight.shape[4]
    total = jnp.zeros((frames, rows, in_ch, cols), jnp.float32)
    for kt in range(3):
        for kh in range(3):
            matrix = weight[kt, kh].reshape(-1, in_ch)
            window = stack[2 - kt : 2 - kt + frames, 2 - kh : 2 - kh + rows]
            total = total + jnp.einsum(
                "mc,fhmw->fhcw", matrix, window, preferred_element_type=jnp.float32
            )
    return total


def taps_weight(grad, padded, frames, rows, cols):
    stack = shifted_stack(padded, cols, (0, 1, 2))
    out_ch = grad.shape[2]
    in_ch = padded.shape[2]
    pieces = []
    for kt in range(3):
        for kh in range(3):
            window = stack[kt : kt + frames, kh : kh + rows]
            block = jnp.einsum("fhow,fhmw->om", grad, window, preferred_element_type=jnp.float32)
            pieces.append(block.reshape(out_ch, 3, in_ch).transpose(1, 0, 2))
    return jnp.stack(pieces).reshape(3, 3, 3, out_ch, in_ch)


def extend_field(field, ahead, depth, width):
    count = field.shape[0]
    piece = field[:depth] if ahead else field[count - depth :]
    step = -1 if ahead else 1
    moved = from_behind(piece, "tm", step)
    if ahead:
        field = jnp.concatenate([field, moved], axis=0)
    else:
        field = jnp.concatenate([moved, field], axis=0)
    grown = with_halo(field, (("height", 1),), width)
    return jnp.pad(grown, ((0, 0), (0, 0), (0, 0), (1, 1)))


def shards(inputs, gain_in, conv_in, gain_mid, conv_mid, conv_skip, scored_grads, scored_frames):
    x_local = inputs[0]
    frames, rows, channels, cols = x_local.shape
    first_frame = lax.axis_index("tm") * frames
    all_rows = rows * lax.axis_size("height")
    scale = 1.0 / math.sqrt(
        inputs.shape[0] * lax.axis_size("dp") * scored_frames.shape[1] * all_rows * cols
    )
    x_ext = extend_field(x_local, False, 2, 1)
    h1_pad = act_norm(x_ext.astype(jnp.float32), gain_in).astype(jnp.bfloat16)
    a1 = taps_forward(h1_pad, conv_in, frames, rows, cols).astype(jnp.bfloat16)
    h2 = act_norm(a1.astype(jnp.float32), gain_mid).astype(jnp.bfloat16)
    h2_pad = extend_field(h2, False, 2, 1)
    span, depth = (frames, 2)
    targets = first_frame + jnp.arange(span, dtype=jnp.int32)
    listed = scored_frames[0]
    chosen = (listed[None, :] == targets[:, None]).astype(jnp.bfloat16)
    placed = jnp.einsum(
        "tj,jhow->thow",
        chosen,
        lax.all_gather(scored_grads, "tm", axis=1, tiled=True)[0],
        preferred_element_type=jnp.float32,
    )
    cot_pad = extend_field(placed.astype(jnp.bfloat16), True, depth, 1)
    cot_own = cot_pad[:frames, 1 : rows + 1, :, 1 : cols + 1]
    grad_mid = scale * taps_weight(cot_own, h2_pad, frames, rows, cols)
    grad_skip = scale * jnp.einsum(
        "fhow,fhcw->oc", cot_own, x_local, preferred_element_type=jnp.float32
    )
    gh2 = taps_input(cot_pad, conv_mid, frames, rows, cols)
    _, pull_mid = jax.vjp(lambda v: act_norm(v, gain_mid), a1.astype(jnp.float32))
    ga1 = pull_mid(gh2)[0].astype(jnp.bfloat16)
    ga1_pad = extend_field(ga1, True, 2, 1)
    grad_first = scale * taps_weight(ga1, h1_pad, frames, rows, cols)
    gh1 = taps_input(ga1_pad, conv_in, frames, rows, cols)
    _, pull_in = jax.vjp(lambda v: act_norm(v, gain_in), x_local.astype(jnp.float32))
    skip_back = jnp.einsum("oc,fhow->fhcw", conv_skip, cot_own, preferred_element_type=jnp.float32)
    grad_inputs = (pull_in(gh1)[0] + skip_back).astype(jnp.bfloat16)[None]
    grad_first, grad_mid, grad_skip = lax.psum(
        (grad_first, grad_mid, grad_skip), ("dp", "tm", "height")
    )
    return (grad_inputs, grad_first, grad_mid, grad_skip)


def solution(mesh):
    in_specs = (
        P("dp", "tm", "height", None, None),
        P(),
        P(),
        P(),
        P(),
        P(),
        P("dp", "tm", "height", None, None),
        P("dp", None),
    )
    out_specs = (P("dp", "tm", "height", None, None), P(), P(), P())
    return jax.shard_map(shards, mesh=mesh, in_specs=in_specs, out_specs=out_specs, check_vma=False)
```

profile of v0, /device:TPU:1, one launch (start us, length us, event | category | flops | bytes accessed | tf_op | source)
XLA Modules:
  0.0 430.9 jit_solution(1858186298045383722)
XLA Ops:
  7.3 26.1 %all_gather.3 = bf16[1,16,2,96,128]{4,3,2,0,1:T(8,128)(2,1)S(1)} all-gather(bf16[1,2,2,96,128]{4,3,2,0,1:T(8,128)(2,1)} %bitcast.396), channel_id=1, replica_groups=mesh['dp'=2,'tm'=8,'height'=16] {'tm'}, dimensions={1}, use_global_device_ids=true | all-gather | bytes 884736 | tf_op jit(solution)/shard_map/all_gather | solution.py:115
  33.3 1.2 convolution_convert_fusion
  34.6 1.3 collective-permute-start
  35.9 1.6 slice_bitcast_fusion
  37.5 4.0 collective-permute-start.3
  41.5 0.9 fusion.60
  42.4 0.8 fusion.144
  43.2 1.2 fusion.141
  44.6 0.9 fusion.116
  45.5 4.4 %collective-permute-start.1 = (bf16[6,1,96,128]{3,0,2,1:T(8,128)(2,1)}, bf16[6,1,96,128]{3,0,2,1:T(8,128)(2,1)S(1)}, u32[]{:S(2)}, u32[]{:S(2)}) collective-permute-start(bf16[6,1,96,128]{3,0,2,1:T(8,128)(2,1)} %get-tuple-element.62), channel_id=1, source_target_pairs={{0,1},{1,2},{2,3},{3,4},{4,5},{5,6},{6,7},{7,8},{8,9},{9,10},{10,1... | collective-permute-start | bytes 442376 | tf_op jit(solution)/shard_map/ppermute | solution.py:23
  49.9 1.3 collective-permute-start.2
  51.2 0.8 copy.163
  52.1 1.1 copy.165
  54.3 5.5 %collective-permute-start.4 = (bf16[6,1,192,128]{3,2,1,0:T(8,128)(2,1)S(1)}, bf16[6,1,192,128]{3,2,1,0:T(8,128)(2,1)S(1)}, u32[]{:S(2)}, u32[]{:S(2)}) collective-permute-start(bf16[6,1,192,128]{3,2,1,0:T(8,128)(2,1)S(1)} %get-tuple-element.54), channel_id=1, source_target_pairs={{0,1},{1,2},{2,3},{3,4},{4,5},{5,6},{6,7},{7,8},{8,9},{9,10},{10,1... | collective-permute-start | bytes 884744 | tf_op jit(solution)/shard_map/ppermute | solution.py:23
  59.8 1.5 collective-permute-start.5
  61.3 1.3 select_maximum_fusion.2
  63.0 6.4 %pad_maximum_fusion.1 = bf16[6,4,288,128]{3,0,2,1:T(8,128)(2,1)S(1)} fusion(bf16[6,4,96,128]{3,0,2,1:T(8,128)(2,1)S(1)} %get-tuple-element.22, bf16[6,1,96,128]{3,0,2,1:T(8,128)(2,1)S(1)} %collective-permute-done.2, bf16[2,2,96,128]{3,0,2,1:T(2,128)(2,1)S(1)} %collective-permute-done, bf16[4,2,96,128]{3,0,2,1:T(4,128)(2,1)S(1)} %convolution_convert_fusion, ...), kind=kLoop, calls=%fused_computation.24 | loop fusion | flops 10616832 | bytes 3538944 | tf_op jit(solution)/shard_map/concatenate | solution.py:38
  69.4 1.9 fusion.138
  74.0 2.3 fusion
  76.3 1.6 fusion.7
  78.0 0.9 fusion.139
  84.0 0.6 multiply_reduce_fusion
  89.0 0.6 slice.350
  89.7 2.8 collective-permute-start.9
  92.5 1.3 collective-permute-start.6
  94.1 0.7 fusion.117
  94.9 6.1 %collective-permute-start.10 = (bf16[6,1,96,128]{3,2,1,0:T(8,128)(2,1)}, bf16[6,1,96,128]{3,2,1,0:T(8,128)(2,1)}, u32[]{:S(2)}, u32[]{:S(2)}) collective-permute-start(bf16[6,1,96,128]{3,2,1,0:T(8,128)(2,1)} %get-tuple-element.58), channel_id=1, source_target_pairs={{0,1},{1,2},{2,3},{3,4},{4,5},{5,6},{6,7},{7,8},{8,9},{9,10},{10,1... | collective-permute-start | bytes 442376 | tf_op jit(solution)/shard_map/ppermute | solution.py:23
  101.0 1.3 collective-permute-start.11
  102.5 2.4 copy.199
  104.9 0.9 fusion.118
  105.8 5.6 %collective-permute-start.7 = (bf16[6,1,96,128]{3,2,1,0:T(8,128)(2,1)S(1)}, bf16[6,1,96,128]{3,2,1,0:T(8,128)(2,1)S(1)}, u32[]{:S(2)}, u32[]{:S(2)}) collective-permute-start(bf16[6,1,96,128]{3,2,1,0:T(8,128)(2,1)S(1)} %get-tuple-element.60), channel_id=1, source_target_pairs={{0,1},{1,2},{2,3},{3,4},{4,5},{5,6},{6,7},{7,8},{8,9},{9,10},{10,1... | collective-permute-start | bytes 442376 | tf_op jit(solution)/shard_map/ppermute | solution.py:23
  111.4 1.6 collective-permute-start.8
  113.0 1.8 select_maximum_fusion.4
  115.1 1.1 pad_maximum_fusion.3
  119.3 1.5 copy.218
  120.8 1.5 select_maximum_fusion.7
  122.6 1.1 pad_maximum_fusion.2
  124.2 1.3 fusion.147
  125.5 1.3 fusion.148
  126.8 1.3 fusion.149
  128.1 1.3 fusion.150
  129.5 0.9 copy-done.15
  132.6 1.0 fusion.71
  133.7 1.1 fusion.27
  134.7 284.0 %all-reduce.7.cloned.1.call-done = (f32[3,3,3,96,192]{4,3,2,1,0:T(8,128)}, f32[3,3,3,96,96]{4,3,2,1,0:T(8,128)}, f32[96,192]{1,0:T(8,128)}) async-done(((f32[3,3,3,96,192]{4,3,2,1,0:T(8,128)}, f32[3,3,3,96,96]{4,3,2,1,0:T(8,128)}, f32[96,192]{1,0:T(8,128)}), (f32[3,3,3,96,192]{4,3,2,1,0:T(8,128)}, f32[3,3,3,96,96]{4,3,2,1,0:T(8,128)}, f32[96,192]{1,0:T(8,128)})) %all-reduce.7.cloned.1.call-update) | async-done | bytes 3059728 | tf_op jit(solution)/shard_map/psum | solution.py:133
  418.7 3.6 copy.381
  422.4 1.1 copy.382
  423.5 0.6 copy.383
  (162 shorter events, 20.4 us)
Async XLA Ops:
  7.2 126.5 %copy-start = (bf16[96,192]{1,0:T(8,128)(2,1)S(1)}, bf16[96,192]{1,0:T(8,128)(2,1)}, u32[]{:S(2)}) copy-start(bf16[96,192]{1,0:T(8,128)(2,1)} %param.13) | copy-start | bytes 110596
  7.2 34.4 %copy-start.1 = (bf16[1,4,2,192,128]{4,3,2,1,0:T(8,128)(2,1)S(1)}, bf16[1,4,2,192,128]{4,3,2,1,0:T(8,128)(2,1)}, u32[]{:S(2)}) copy-start(bf16[1,4,2,192,128]{4,3,2,1,0:T(8,128)(2,1)} %param.8) | copy-start | bytes 1179652
  7.2 35.2 %copy-start.12 = (bf16[3,3,3,96,96]{4,3,2,1,0:T(8,128)(2,1)S(1)}, bf16[3,3,3,96,96]{4,3,2,1,0:T(8,128)(2,1)}, u32[]{:S(2)}) copy-start(bf16[3,3,3,96,96]{4,3,2,1,0:T(8,128)(2,1)} %param.12) | copy-start | bytes 1492996
  7.2 36.0 %copy-start.9 = (bf16[3,3,3,96,192]{4,3,2,1,0:T(8,128)(2,1)S(1)}, bf16[3,3,3,96,192]{4,3,2,1,0:T(8,128)(2,1)}, u32[]{:S(2)}) copy-start(bf16[3,3,3,96,192]{4,3,2,1,0:T(8,128)(2,1)} %param.10) | copy-start | bytes 2985988
  7.2 411.5 %all-reduce.7.cloned.1.call-start = ((), (), s32[]{:S(2)}) async-start(), calls=%async_computation | async-start | bytes 8159232 | tf_op jit(solution)/shard_map/psum | solution.py:133
  34.6 9.9 %collective-permute-start = (bf16[2,2,96,128]{3,0,2,1:T(2,128)(2,1)S(1)}, bf16[2,2,96,128]{3,0,2,1:T(2,128)(2,1)S(1)}, u32[]{:S(2)}, u32[]{:S(2)}) collective-permute-start(bf16[2,2,96,128]{3,0,2,1:T(2,128)(2,1)S(1)} %slice.331), channel_id=1, source_target_pairs={{16,0},{32,16},{48,32},{64,48},{80,64},{96,80},{112,96},{17,1},{33... | collective-permute-start | bytes 294920 | tf_op jit(solution)/shard_map/ppermute | solution.py:12
  37.5 16.7 %collective-permute-start.3 = (bf16[2,2,192,128]{3,2,1,0:T(8,128)(2,1)}, bf16[2,2,192,128]{3,2,1,0:T(8,128)(2,1)S(1)}, u32[]{:S(2)}, u32[]{:S(2)}) collective-permute-start(bf16[2,2,192,128]{3,2,1,0:T(8,128)(2,1)} %slice_bitcast_fusion), channel_id=1, source_target_pairs={{0,16},{16,32},{32,48},{48,64},{64,80},{80,96},{96,112},{1,17},{17... | collective-permute-start | bytes 589832 | tf_op jit(solution)/shard_map/ppermute | solution.py:12
  45.5 15.8 %collective-permute-start.1 = (bf16[6,1,96,128]{3,0,2,1:T(8,128)(2,1)}, bf16[6,1,96,128]{3,0,2,1:T(8,128)(2,1)S(1)}, u32[]{:S(2)}, u32[]{:S(2)}) collective-permute-start(bf16[6,1,96,128]{3,0,2,1:T(8,128)(2,1)} %get-tuple-element.62), channel_id=1, source_target_pairs={{0,1},{1,2},{2,3},{3,4},{4,5},{5,6},{6,7},{7,8},{8,9},{9,10},{10,1... | collective-permute-start | bytes 442376 | tf_op jit(solution)/shard_map/ppermute | solution.py:23
  49.9 11.4 %collective-permute-start.2 = (bf16[6,1,96,128]{3,0,2,1:T(8,128)(2,1)}, bf16[6,1,96,128]{3,0,2,1:T(8,128)(2,1)S(1)}, u32[]{:S(2)}, u32[]{:S(2)}) collective-permute-start(bf16[6,1,96,128]{3,0,2,1:T(8,128)(2,1)} %get-tuple-element.63), channel_id=1, source_target_pairs={{1,0},{2,1},{3,2},{4,3},{5,4},{6,5},{7,6},{8,7},{9,8},{10,9},{11,1... | collective-permute-start | bytes 442376 | tf_op jit(solution)/shard_map/ppermute | solution.py:25
  54.3 19.7 %collective-permute-start.4 = (bf16[6,1,192,128]{3,2,1,0:T(8,128)(2,1)S(1)}, bf16[6,1,192,128]{3,2,1,0:T(8,128)(2,1)S(1)}, u32[]{:S(2)}, u32[]{:S(2)}) collective-permute-start(bf16[6,1,192,128]{3,2,1,0:T(8,128)(2,1)S(1)} %get-tuple-element.54), channel_id=1, source_target_pairs={{0,1},{1,2},{2,3},{3,4},{4,5},{5,6},{6,7},{7,8},{8,9},{9,10},{10,1... | collective-permute-start | bytes 884744 | tf_op jit(solution)/shard_map/ppermute | solution.py:23
  59.8 14.2 %collective-permute-start.5 = (bf16[6,1,192,128]{3,2,1,0:T(8,128)(2,1)S(1)}, bf16[6,1,192,128]{3,2,1,0:T(8,128)(2,1)S(1)}, u32[]{:S(2)}, u32[]{:S(2)}) collective-permute-start(bf16[6,1,192,128]{3,2,1,0:T(8,128)(2,1)S(1)} %get-tuple-element.55), channel_id=1, source_target_pairs={{1,0},{2,1},{3,2},{4,3},{5,4},{6,5},{7,6},{8,7},{9,8},{10,9},{11,1... | collective-permute-start | bytes 884744 | tf_op jit(solution)/shard_map/ppermute | solution.py:25
  69.4 1.9 copy-start.29
  69.4 2.3 copy-start.28
  69.4 2.6 copy-start.27
  71.3 1.0 copy-start.26
  71.3 1.3 copy-start.25
  71.7 1.3 copy-start.24
  72.0 1.3 copy-start.23
  73.6 2.7 copy-start.32
  78.9 0.9 copy-start.21
  83.1 0.9 copy-start.30
  83.1 0.9 copy-start.33
  84.8 9.3 %copy-start.2 = (bf16[4,2,96,128]{3,2,1,0:T(8,128)(2,1)}, bf16[4,2,96,128]{3,2,1,0:T(8,128)(2,1)S(1)}, u32[]{:S(2)}) copy-start(bf16[4,2,96,128]{3,2,1,0:T(8,128)(2,1)S(1)} %get-tuple-element.56) | copy-start | bytes 589828
  89.7 4.4 %collective-permute-start.9 = (bf16[2,2,96,128]{3,2,1,0:T(8,128)(2,1)S(1)}, bf16[2,2,96,128]{3,2,1,0:T(8,128)(2,1)S(1)}, u32[]{:S(2)}, u32[]{:S(2)}) collective-permute-start(bf16[2,2,96,128]{3,2,1,0:T(8,128)(2,1)S(1)} %slice.364), channel_id=1, source_target_pairs={{0,16},{16,32},{32,48},{48,64},{64,80},{80,96},{96,112},{1,17},{17... | collective-permute-start | bytes 294920 | tf_op jit(solution)/shard_map/ppermute | solution.py:12
  92.5 12.4 %collective-permute-start.6 = (bf16[2,2,96,128]{3,2,1,0:T(8,128)(2,1)}, bf16[2,2,96,128]{3,2,1,0:T(8,128)(2,1)}, u32[]{:S(2)}, u32[]{:S(2)}) collective-permute-start(bf16[2,2,96,128]{3,2,1,0:T(8,128)(2,1)} %slice.350), channel_id=1, source_target_pairs={{16,0},{32,16},{48,32},{64,48},{80,64},{96,80},{112,96},{17,1},{33... | collective-permute-start | bytes 294920 | tf_op jit(solution)/shard_map/ppermute | solution.py:12
  94.1 6.9 %copy-start.10 = (bf16[2,2,96,128]{3,2,1,0:T(8,128)(2,1)}, bf16[2,2,96,128]{3,2,1,0:T(8,128)(2,1)S(1)}, u32[]{:S(2)}) copy-start(bf16[2,2,96,128]{3,2,1,0:T(8,128)(2,1)S(1)} %collective-permute-done.9) | copy-start | bytes 294916
  94.9 18.1 %collective-permute-start.10 = (bf16[6,1,96,128]{3,2,1,0:T(8,128)(2,1)}, bf16[6,1,96,128]{3,2,1,0:T(8,128)(2,1)}, u32[]{:S(2)}, u32[]{:S(2)}) collective-permute-start(bf16[6,1,96,128]{3,2,1,0:T(8,128)(2,1)} %get-tuple-element.58), channel_id=1, source_target_pairs={{0,1},{1,2},{2,3},{3,4},{4,5},{5,6},{6,7},{7,8},{8,9},{9,10},{10,1... | collective-permute-start | bytes 442376 | tf_op jit(solution)/shard_map/ppermute | solution.py:23
  101.0 12.0 %collective-permute-start.11 = (bf16[6,1,96,128]{3,2,1,0:T(8,128)(2,1)}, bf16[6,1,96,128]{3,2,1,0:T(8,128)(2,1)}, u32[]{:S(2)}, u32[]{:S(2)}) collective-permute-start(bf16[6,1,96,128]{3,2,1,0:T(8,128)(2,1)} %get-tuple-element.59), channel_id=1, source_target_pairs={{1,0},{2,1},{3,2},{4,3},{5,4},{6,5},{7,6},{8,7},{9,8},{10,9},{11,1... | collective-permute-start | bytes 442376 | tf_op jit(solution)/shard_map/ppermute | solution.py:25
  104.9 10.1 %copy-start.3 = (bf16[4,2,96,128]{3,2,1,0:T(8,128)(2,1)S(1)}, bf16[4,2,96,128]{3,2,1,0:T(8,128)(2,1)}, u32[]{:S(2)}) copy-start(bf16[4,2,96,128]{3,2,1,0:T(8,128)(2,1)} %copy-done.2) | copy-start | bytes 589828
  104.9 10.1 %copy-start.11 = (bf16[2,2,96,128]{3,2,1,0:T(8,128)(2,1)S(1)}, bf16[2,2,96,128]{3,2,1,0:T(8,128)(2,1)}, u32[]{:S(2)}) copy-start(bf16[2,2,96,128]{3,2,1,0:T(8,128)(2,1)} %copy-done.10) | copy-start | bytes 294916
  105.8 15.0 %collective-permute-start.7 = (bf16[6,1,96,128]{3,2,1,0:T(8,128)(2,1)S(1)}, bf16[6,1,96,128]{3,2,1,0:T(8,128)(2,1)S(1)}, u32[]{:S(2)}, u32[]{:S(2)}) collective-permute-start(bf16[6,1,96,128]{3,2,1,0:T(8,128)(2,1)S(1)} %get-tuple-element.60), channel_id=1, source_target_pairs={{0,1},{1,2},{2,3},{3,4},{4,5},{5,6},{6,7},{7,8},{8,9},{9,10},{10,1... | collective-permute-start | bytes 442376 | tf_op jit(solution)/shard_map/ppermute | solution.py:23
  111.4 9.4 %collective-permute-start.8 = (bf16[6,1,96,128]{3,2,1,0:T(8,128)(2,1)S(1)}, bf16[6,1,96,128]{3,2,1,0:T(8,128)(2,1)S(1)}, u32[]{:S(2)}, u32[]{:S(2)}) collective-permute-start(bf16[6,1,96,128]{3,2,1,0:T(8,128)(2,1)S(1)} %get-tuple-element.61), channel_id=1, source_target_pairs={{1,0},{2,1},{3,2},{4,3},{5,4},{6,5},{7,6},{8,7},{9,8},{10,9},{11,1... | collective-permute-start | bytes 442376 | tf_op jit(solution)/shard_map/ppermute | solution.py:25
  122.6 1.1 copy-start.20
  122.6 1.5 copy-start.19
  123.7 1.8 copy-start.18
  124.2 2.7 copy-start.17
  125.5 2.6 copy-start.16
  129.4 0.9 copy-start.15
  129.4 1.4 copy-start.14
  129.4 1.8 copy-start.13
  130.7 1.1 copy-start.4
  130.7 1.4 copy-start.5
  130.8 1.6 copy-start.6
  130.8 1.8 copy-start.7
  130.8 1.8 copy-start.22
  418.7 3.6 copy-start.8
  422.4 1.1 copy-start.31
Sparse Core Ops, SparseCore 0:
  129.6 289.1 all-reduce.6
where the time goes:
time: 433 us; the launch traced here: 431 us
  waiting for transfers between devices  284 us (66%)
  starting transfers between devices  36.6 us (8%)
  blocking collectives  26.1 us (6%)
  matrix products  24.6 us (6%)
  local copies, waits for them, and re-layouts  23.4 us (5%)
  other arithmetic  21 us (5%)
  between operations  15.1 us (3%)
    psum x1, waiting for transfers between devices, shards(): lax.psum((grad_first, grad_mid, grad_skip), ('dp', 'tm', 'height'))  284 us
    all_gather x1, blocking collectives, shards(): lax.all_gather(scored_grads, 'tm', axis=1, tiled=True)[0]  26.1 us
    ppermute x4, starting transfers between devices, with_halo(): lax.ppermute(tail, axis, [(i, (i + 1) % count) for i in range(ends)])  21.6 us
    dot_general x18, matrix products, taps_input(): jnp.einsum('mc,fhmw->fhcw', matrix, window, preferred_element_type=jnp.fl...  11 us
    ppermute x4, starting transfers between devices, from_behind(): lax.ppermute(value, axis, [(source, source + steps) for source in range(l...  9.39 us
    concatenate x4, other arithmetic, shifted_stack(): return jnp.concatenate([padded[..., k:k + cols] for k in offsets], axis=2)  9.08 us
  transfers between devices with their start and end apart: 13, of which 1 were waited for; matrix products, arithmetic and copies ran while one was open for 8% of the time, Pallas kernels for 0%

commit v1 on v0

v1 whole, which is shorter than its diff:
```python
import math

import jax
import jax.numpy as jnp
from jax import lax
from jax.experimental import pallas as pl
from jax.experimental.pallas import tpu as pltpu
from jax.sharding import PartitionSpec as P

MESH = pl.DeviceIdType.MESH
F32 = jnp.float32
BF16 = jnp.bfloat16
FR, RW, CI, CO, W = 4, 2, 192, 96, 128
TM, HT = 8, 16
SC = 2
EPS = 1e-06
TAPS = [(kt, kh) for kt in range(3) for kh in range(3)]
PAIRS = [(0, 1), (2, 3), (4, 5), (6, 7)]
ROWS_IN, ROWS_MID = 4096, 2048


def sigmoid(u):
    return 1.0 / (1.0 + jnp.exp(-u))


def norm_parts(v, g):
    s = lax.rsqrt(jnp.mean(v * v, axis=0, keepdims=True) + EPS)
    n = v * s
    u = n * g
    return s, n, u, sigmoid(u)


def norm_fwd(v, g):
    _, _, u, sg = norm_parts(v, g)
    return u * sg


def norm_pull(v, g, ct):
    s, n, u, sg = norm_parts(v, g)
    dn = ct * (sg * (1.0 + u * (1.0 - sg))) * g
    return s * (dn - n * jnp.mean(dn * n, axis=0, keepdims=True))


def ahead(v):
    lane = lax.broadcasted_iota(jnp.int32, v.shape, 1)
    return jnp.where(lane == W - 1, 0.0, pltpu.roll(v, W - 1, 1))


def behind(v):
    lane = lax.broadcasted_iota(jnp.int32, v.shape, 1)
    return jnp.where(lane == 0, 0.0, pltpu.roll(v, 1, 1))


def column(row, n):
    r = lax.broadcasted_iota(jnp.int32, (n, n), 0)
    c = lax.broadcasted_iota(jnp.int32, (n, n), 1)
    return jnp.sum(jnp.where(r == c, jnp.broadcast_to(row, (n, n)), 0.0), axis=1, keepdims=True)


def dot(a, b):
    return jnp.dot(a, b, preferred_element_type=F32)


def dot_nt(a, b):
    return lax.dot_general(a, b, (((1,), (1,)), ((), ())), preferred_element_type=F32)


def pair(ref, f, r):
    return jnp.concatenate([ref[f, r], ref[f, r + 1]], axis=1)


class Sems:
    def __init__(self, send, recv):
        self.send, self.recv, self.n = send, recv, 0

    def take(self, count):
        at = self.n
        self.n += count
        return list(range(at, at + count))


N_SEMS = 120
N_LOCAL = 8


def when(cond, fn):
    if cond is None:
        fn()
    else:
        pl.when(cond)(fn)


def kernel(scale, sf, x_hbm, gain_in, win_hbm, gain_mid, wmid_hbm, wskip, sg_hbm,
           out_x, out_in, out_mid, out_skip,
           XE, H1, SG, CE, CS, GE, GS, A1, H2, WIN, WMID, WTI, WTM,
           g_in, g_mid, rc_in, rc_mid, s_in, s_mid,
           a1_in, b1_in, a1_mid, b1_mid, p_in, p_mid, a2_in, b2_in, a2_mid, b2_mid,
           c_in, c_mid, z_in, z_mid, fin_in, fin_mid,
           send, recv, local):
    c = lax.axis_index("dp")
    t = lax.axis_index("tm")
    h = lax.axis_index("height")
    y, x_lo = t % 4, t // 4
    z, x_hi = h // 2, h % 2
    xx = x_hi * 2 + x_lo
    sems = Sems(send, recv)
    sent = []

    def dev(tt=None, hh=None, cc=None):
        d = {}
        d["dp"] = c if cc is None else cc
        d["tm"] = t if tt is None else tt
        d["height"] = h if hh is None else hh
        return d

    def x_peer(v):
        return dev(tt=y + 4 * (v % 2), hh=z * 2 + v // 2)

    def y_peer(v):
        return dev(tt=x_lo * 4 + v)

    def z_peer(v):
        return dev(hh=v * 2 + x_hi)

    class Copy:
        def __init__(self, src, dst, to, s_if=None, r_if=None):
            i = sems.take(1)[0]
            self.d = pltpu.make_async_remote_copy(
                src_ref=src, dst_ref=dst, send_sem=send.at[i], recv_sem=recv.at[i],
                device_id=to, device_id_type=MESH)
            self.s_if, self.r_if = s_if, r_if

        def start(self):
            when(self.s_if, lambda: self.d.start())
            sent.append(self)

        def got(self):
            when(self.r_if, lambda: self.d.wait_recv())

        def left(self):
            when(self.s_if, lambda: self.d.wait_send())

    loc = [
        pltpu.make_async_copy(x_hbm.at[0], XE.at[pl.ds(2, FR), pl.ds(1, RW)], local.at[0]),
        pltpu.make_async_copy(sg_hbm.at[0], SG.at[pl.ds(SC * t, SC)], local.at[1]),
        pltpu.make_async_copy(win_hbm, WIN, local.at[2]),
        pltpu.make_async_copy(wmid_hbm, WMID, local.at[3]),
    ]
    for item in loc:
        item.start()

    barrier = pltpu.get_barrier_semaphore()
    friends = [dev(tt=(t + k) % TM) for k in range(1, TM)]
    friends += [dev(hh=(h + k) % HT) for k in (1, 15, 2, 4, 6, 8, 10, 12, 14)]
    friends += [dev(tt=(t + a) % TM, hh=(h + b) % HT) for a in (1, 7) for b in (1, 15)]
    friends += [x_peer(3 - xx), dev(cc=1 - c)]
    for to in friends:
        pl.semaphore_signal(barrier, inc=1, device_id=to, device_id_type=MESH)

    first_t, last_t, first_h, last_h = t == 0, t == TM - 1, h == 0, h == HT - 1

    def zero(ref, f0, nf, r0, nr, ch):
        def body():
            for f in range(f0, f0 + nf):
                for r in range(r0, r0 + nr):
                    ref[f, r] = jnp.zeros((ch, W), BF16)
        return body

    pl.when(first_t)(zero(XE, 0, 2, 0, 4, CI))
    pl.when(jnp.logical_and(first_h, t > 0))(zero(XE, 0, 2, 0, 1, CI))
    pl.when(jnp.logical_and(last_h, t > 0))(zero(XE, 0, 2, 3, 1, CI))
    pl.when(first_h)(zero(XE, 2, 4, 0, 1, CI))
    pl.when(last_h)(zero(XE, 2, 4, 3, 1, CI))
    pl.when(first_h)(zero(CE, 0, 6, 0, 1, CO))
    pl.when(last_h)(zero(CE, 0, 6, 3, 1, CO))
    pl.when(last_t)(zero(GE, 4, 2, 0, 4, CO))
    pl.when(jnp.logical_and(first_h, t < TM - 1))(zero(GE, 4, 2, 0, 1, CO))
    pl.when(jnp.logical_and(last_h, t < TM - 1))(zero(GE, 4, 2, 3, 1, CO))
    pl.when(first_h)(zero(GE, 0, 4, 0, 1, CO))
    pl.when(last_h)(zero(GE, 0, 4, 3, 1, CO))

    pl.semaphore_wait(barrier, len(friends))

    both = jnp.logical_and
    has_n, has_p = h < HT - 1, h > 0
    t_n, t_p = t < TM - 1, t > 0

    gather = [
        Copy(sg_hbm.at[0], SG.at[pl.ds(SC * t, SC)], dev(tt=(t + k) % TM)) for k in (1, 7, 2, 6, 3, 5, 4)
    ]
    for item in gather:
        item.start()

    src = x_hbm.at[0]
    x_halo = [
        Copy(src.at[:, 1], XE.at[pl.ds(2, 4), 0], dev(hh=h + 1), has_n, has_p),
        Copy(src.at[:, 0], XE.at[pl.ds(2, 4), 3], dev(hh=h - 1), has_p, has_n),
        Copy(src.at[pl.ds(2, 2)], XE.at[pl.ds(0, 2), pl.ds(1, 2)], dev(tt=t + 1), t_n, t_p),
        Copy(src.at[pl.ds(2, 2), 1], XE.at[pl.ds(0, 2), 0], dev(tt=t + 1, hh=h + 1),
             both(t_n, has_n), both(t_p, has_p)),
        Copy(src.at[pl.ds(2, 2), 0], XE.at[pl.ds(0, 2), 3], dev(tt=t + 1, hh=h - 1),
             both(t_n, has_p), both(t_p, has_n)),
    ]
    for item in x_halo:
        item.start()

    g1 = column(gain_in[...], CI)
    g2 = column(gain_mid[...], CO)

    def h1_at(f, r):
        H1[f, r] = norm_fwd(XE[f, r].astype(F32), g1).astype(BF16)

    loc[2].wait()
    loc[3].wait()

    def turn(i, _):
        kt, kh, kw = i // 9, (i // 3) % 3, i % 3
        WTI[i] = WIN[kt, kh, kw].astype(F32).T.astype(BF16)
        WTM[i] = WMID[kt, kh, kw].astype(F32).T.astype(BF16)
        return 0

    lax.fori_loop(0, 27, turn, 0)
    loc[0].wait()

    def h1_own(i, _):
        h1_at(2 + i // 2, 1 + i % 2)
        return 0

    lax.fori_loop(0, 8, h1_own, 0)

    loc[1].wait()
    for item in gather:
        item.got()
    for f in range(6):
        frame = t * FR + f
        at = jnp.int32(0)
        found = jnp.int32(0)
        for j in range(SC * TM):
            hit = (sf[0, j] == frame).astype(jnp.int32)
            at = jnp.maximum(at, j * hit)
            found = jnp.maximum(found, hit)
        factor = found.astype(F32)
        for r in range(RW):
            CE[f, 1 + r] = (SG[at, r].astype(F32) * factor).astype(BF16)
    cot_halo = [
        Copy(CE.at[:, 2], CE.at[:, 0], dev(hh=h + 1), has_n, has_p),
        Copy(CE.at[:, 1], CE.at[:, 3], dev(hh=h - 1), has_p, has_n),
    ]
    for item in cot_halo:
        item.start()

    skip_a = jnp.zeros((CO, W), F32)
    skip_b = jnp.zeros((CO, W), F32)
    for f in range(FR):
        cot = pair(CE, f, 1)
        xs = pair(XE, 2 + f, 1)
        skip_a = skip_a + dot_nt(cot, xs[:W])
        skip_b = skip_b + dot_nt(cot, jnp.concatenate([jnp.zeros((64, 2 * W), BF16), xs[W:]], axis=0))
    g_mid[pl.ds(2016, 32)] = skip_a[:32].astype(BF16)
    g_in[pl.ds(4032, 64)] = skip_a[32:].astype(BF16)

    for item in x_halo:
        item.got()

    def h1_rows(f, _):
        h1_at(f, 0)
        h1_at(f, 3)
        return 0

    def h1_prior(f, _):
        h1_at(f, 1)
        h1_at(f, 2)
        return 0

    lax.fori_loop(0, 6, h1_rows, 0)
    lax.fori_loop(0, 2, h1_prior, 0)

    def forward(f, _):
        acc = jnp.zeros((3 * CO, 2 * W), F32)
        for kt, kh in TAPS:
            acc = acc + dot(WIN[kt, kh].reshape(3 * CO, CI), pair(H1, f + kt, kh))
        for r in range(RW):
            part = acc[:, r * W:(r + 1) * W]
            a1 = part[CO:2 * CO] + behind(part[:CO]) + ahead(part[2 * CO:])
            a1 = a1.astype(BF16)
            A1[f, r] = a1
            H2[f, r] = norm_fwd(a1.astype(F32), g2).astype(BF16)
        return 0

    lax.fori_loop(0, FR, forward, 0)

    for item in cot_halo:
        item.got()

    def back_mid(f, _):
        acc = jnp.zeros((3 * CO, 2 * W), F32)
        for n, (kt, kh) in enumerate(TAPS):
            acc = acc + dot(WTM[pl.ds(3 * n, 3)].reshape(3 * CO, CO), pair(CE, f + 2 - kt, 2 - kh))
        for r in range(RW):
            part = acc[:, r * W:(r + 1) * W]
            gh2 = part[CO:2 * CO] + ahead(part[:CO]) + behind(part[2 * CO:])
            ga1 = norm_pull(A1[f, r].astype(F32), g2, gh2).astype(BF16)
            GE[f, 1 + r] = ga1
            wide = ga1.astype(F32)
            lanes = pl.ds(r * W, W)
            GS[f, pl.ds(0, CO), lanes] = ahead(wide).astype(BF16)
            GS[f, pl.ds(CO, CO), lanes] = ga1
            GS[f, pl.ds(2 * CO, CO), lanes] = behind(wide).astype(BF16)
        return 0

    lax.fori_loop(0, FR, back_mid, 0)
    ga_halo = [
        Copy(GE.at[pl.ds(0, 4), 2], GE.at[pl.ds(0, 4), 0], dev(hh=h + 1), has_n, has_p),
        Copy(GE.at[pl.ds(0, 4), 1], GE.at[pl.ds(0, 4), 3], dev(hh=h - 1), has_p, has_n),
        Copy(GE.at[pl.ds(0, 2), pl.ds(1, 2)], GE.at[pl.ds(4, 2), pl.ds(1, 2)], dev(tt=t - 1), t_p, t_n),
        Copy(GE.at[pl.ds(0, 2), 2], GE.at[pl.ds(4, 2), 0], dev(tt=t - 1, hh=h + 1),
             both(t_p, has_n), both(t_n, has_p)),
        Copy(GE.at[pl.ds(0, 2), 1], GE.at[pl.ds(4, 2), 3], dev(tt=t - 1, hh=h - 1),
             both(t_p, has_p), both(t_n, has_n)),
    ]
    for item in ga_halo:
        item.start()

    for n, taps in enumerate(PAIRS):
        acc = jnp.zeros((3 * CO, 3 * W), F32)
        for f in range(FR):
            one = [pair(H1, f + TAPS[i][0], TAPS[i][1]) for i in taps]
            rhs = jnp.concatenate([one[0][:W], one[1][:W], one[0][W:], one[1][W:]], axis=0)
            acc = acc + dot_nt(GS[f], rhs)
        for j in range(3):
            g_in[pl.ds(864 * n + 288 * j, 288)] = acc[:, j * W:(j + 1) * W].astype(BF16)
    acc = jnp.zeros((3 * CO, 2 * W), F32)
    for f in range(FR):
        one = pair(H1, f + 2, 2)
        rhs = jnp.concatenate([one, jnp.zeros((64, 2 * W), BF16)], axis=0)
        acc = acc + dot_nt(GS[f], rhs)
    for j in range(2):
        g_in[pl.ds(3456 + 288 * j, 288)] = acc[:, j * W:(j + 1) * W].astype(BF16)

    def reduce(g, rc, s, a1, b1, p, a2, b2, cc, zz, fin, rows):
        half = rows // 2
        ha = half // 2
        q = ha // 4
        e = q // 4
        owners = 2 * e // 16
        mine = pl.multiple_of(c * half, half)
        other = pl.multiple_of((1 - c) * half, half)

        def at(off, n):
            return pl.ds(pl.multiple_of(off, 16), n)

        def total(terms):
            out = terms[0].astype(F32)
            for term in terms[1:]:
                out = out + term.astype(F32)
            return out.astype(BF16)

        step = 128

        core = Copy(g.at[pl.ds(other, half)], rc, dev(cc=1 - c))
        core.start()
        yield
        core.got()

        def add_core(i, _):
            o = pl.multiple_of(i * step, step)
            s[pl.ds(o, step)] = total([g[pl.ds(pl.multiple_of(mine + o, step), step)], rc[pl.ds(o, step)]])
            return 0

        lax.fori_loop(0, half // step, add_core, 0)
        one = []
        for k in (1, 3, 2):
            xp, yp = (xx + k) % 4, (y + k) % 4
            one.append(Copy(s.at[at(xp * q, q)], a1.at[k - 1], x_peer(xp)))
            one.append(Copy(s.at[at(ha + yp * q, q)], b1.at[k - 1], y_peer(yp)))
        for item in one:
            item.start()
        yield
        for item in one:
            item.got()
        p[pl.ds(0, q)] = total([s[at(xx * q, q)], a1[0], a1[1], a1[2]])
        p[pl.ds(q, q)] = total([s[at(ha + y * q, q)], b1[0], b1[1], b1[2]])
        two = []
        for k in (1, 3, 2):
            xp, yp = (xx + k) % 4, (y + k) % 4
            two.append(Copy(p.at[at(yp * e, e)], a2.at[k - 1], y_peer(yp)))
            two.append(Copy(p.at[at(q + xp * e, e)], b2.at[k - 1], x_peer(xp)))
        for item in two:
            item.start()
        yield
        for item in two:
            item.got()
        cc[pl.ds(0, e)] = total([p[at(y * e, e)], a2[0], a2[1], a2[2]])
        cc[pl.ds(e, e)] = total([p[at(q + xx * e, e)], b2[0], b2[1], b2[2]])
        ks = (1, 7, 2, 6, 3, 5, 4)
        own = None if owners == 8 else z < owners
        three = []
        for k in ks:
            zp = (z + k) % 8
            three.append(Copy(cc.at[at(zp % owners * 16, 16)], zz.at[k - 1], z_peer(zp),
                              None if owners == 8 else zp < owners, own))
        for item in three:
            item.start()
        yield
        for item in three:
            item.got()
        chain_b = (z >= owners // 2).astype(jnp.int32)
        zt = z % (owners // 2)
        base_a = mine + xx * q + y * e
        base_b = mine + ha + y * q + xx * e
        place = base_a + chain_b * (base_b - base_a) + zt * 16

        def finish():
            fin[at(place, 16)] = total([cc[at(z % owners * 16, 16)]] + [zz[k] for k in range(7)])

        when(own, finish)
        four = []
        for k in ks:
            zp, zm = (z + k) % 8, (z + 8 - k) % 8
            four.append(Copy(fin.at[at(place, 16)], fin.at[at(place, 16)], z_peer(zp),
                             own, None if owners == 8 else zm < owners))
        for item in four:
            item.start()
        yield
        for item in four:
            item.got()
        five = []
        for k in (1, 3, 2):
            xp, yp = (xx + k) % 4, (y + k) % 4
            five.append(Copy(fin.at[at(base_a, e)], fin.at[at(base_a, e)], y_peer(yp)))
            five.append(Copy(fin.at[at(base_b, e)], fin.at[at(base_b, e)], x_peer(xp)))
        for item in five:
            item.start()
        yield
        for item in five:
            item.got()
        six = []
        for k in (1, 3, 2):
            xp, yp = (xx + k) % 4, (y + k) % 4
            six.append(Copy(fin.at[at(mine + xx * q, q)], fin.at[at(mine + xx * q, q)], x_peer(xp)))
            six.append(Copy(fin.at[at(mine + ha + y * q, q)], fin.at[at(mine + ha + y * q, q)], y_peer(yp)))
        for item in six:
            item.start()
        yield
        for item in six:
            item.got()
        last = Copy(fin.at[pl.ds(mine, half)], fin.at[pl.ds(mine, half)], dev(cc=1 - c))
        last.start()
        yield
        last.got()
        yield

    big = reduce(g_in, rc_in, s_in, a1_in, b1_in, p_in, a2_in, b2_in, c_in, z_in, fin_in, ROWS_IN)
    small = reduce(g_mid, rc_mid, s_mid, a1_mid, b1_mid, p_mid, a2_mid, b2_mid, c_mid, z_mid, fin_mid, ROWS_MID)
    next(big)

    def cot_shift(f, _):
        for r in range(4):
            wide = CE[f, r].astype(F32)
            lanes = pl.ds(r * W, W)
            CS[f, pl.ds(0, CO), lanes] = ahead(wide).astype(BF16)
            CS[f, pl.ds(CO, CO), lanes] = CE[f, r]
            CS[f, pl.ds(2 * CO, CO), lanes] = behind(wide).astype(BF16)
        return 0

    lax.fori_loop(0, 6, cot_shift, 0)

    def cot_window(f, tap):
        kt, kh = TAPS[tap]
        return CS[f + 2 - kt, :, pl.ds((2 - kh) * W, 2 * W)]

    for n in range(2):
        acc = jnp.zeros((CO, 9 * W), F32)
        for f in range(FR):
            rhs = jnp.concatenate([cot_window(f, 4 * n + i) for i in range(4)], axis=0)
            acc = acc + dot_nt(pair(H2, f, 0), rhs)
        for j in range(9):
            g_mid[pl.ds(864 * n + CO * j, CO)] = acc[:, j * W:(j + 1) * W].astype(BF16)
    acc = jnp.zeros((CO, 3 * W), F32)
    for f in range(FR):
        rhs = jnp.concatenate([cot_window(f, 8), jnp.zeros((CO, 2 * W), BF16)], axis=0)
        acc = acc + dot_nt(pair(H2, f, 0), rhs)
    g_mid[pl.ds(1728, CO)] = acc[:, :W].astype(BF16)
    g_mid[pl.ds(1824, CO)] = acc[:, W:2 * W].astype(BF16)
    g_mid[pl.ds(1920, CO)] = (acc[:, 2 * W:] + skip_b).astype(BF16)

    next(small)
    next(big)
    next(small)

    def back_in(f):
        acc = jnp.zeros((3 * CI, 2 * W), F32)
        for n, (kt, kh) in enumerate(TAPS):
            acc = acc + dot(WTI[pl.ds(3 * n, 3)].reshape(3 * CI, CO), pair(GE, f + 2 - kt, 2 - kh))
        skip = lax.dot_general(wskip[...], pair(CE, f, 1), (((0,), (0,)), ((), ())),
                               preferred_element_type=F32)
        for r in range(RW):
            part = acc[:, r * W:(r + 1) * W]
            gh1 = part[CI:2 * CI] + ahead(part[:CI]) + behind(part[2 * CI:])
            grad = norm_pull(XE[2 + f, 1 + r].astype(F32), g1, gh1) + skip[:, r * W:(r + 1) * W]
            out_x[0, f, r] = grad.astype(BF16)

    for item in ga_halo:
        item.got()
    for f in range(FR):
        back_in(f)
        next(big)
        next(small)
    for _ in range(2):
        next(big)
        next(small)
    next(big)

    for n, taps in enumerate(PAIRS):
        for kw in range(3):
            low = fin_in[pl.ds(864 * n + 576 + CO * kw, CO)].astype(F32) * scale
            for j, i in enumerate(taps):
                kt, kh = TAPS[i]
                high = fin_in[pl.ds(864 * n + 288 * j + CO * kw, CO)].astype(F32) * scale
                out_in[kt, kh, kw, :, pl.ds(0, W)] = high
                rest = low if j == 0 else pltpu.roll(low, 64, 1)
                out_in[kt, kh, kw, :, pl.ds(W, 64)] = rest[:, :64]
    for kw in range(3):
        out_in[2, 2, kw, :, pl.ds(0, W)] = fin_in[pl.ds(3456 + CO * kw, CO)].astype(F32) * scale
        out_in[2, 2, kw, :, pl.ds(W, 64)] = (fin_in[pl.ds(3744 + CO * kw, CO)].astype(F32) * scale)[:, :64]
    out_skip[pl.ds(32, 64), pl.ds(0, W)] = fin_in[pl.ds(4032, 64)].astype(F32) * scale
    next(small)
    for j in range(20):
        out_mid[pl.ds(W * j, W)] = (fin_mid[pl.ds(CO * j, CO)].astype(F32) * scale).T
    tail = fin_mid[pl.ds(1920, CO)].astype(F32) * scale
    out_mid[pl.ds(2560, 32)] = tail.T[:32]
    out_skip[:, pl.ds(W, 64)] = pltpu.roll(tail, 64, 1)[:, :64]
    out_skip[pl.ds(0, 32), pl.ds(0, W)] = fin_mid[pl.ds(2016, 32)].astype(F32) * scale

    for item in sent:
        item.left()


def reduce_scratch(rows):
    half = rows // 2
    q, e = half // 8, half // 32
    return {
        "g": (rows, W), "rc": (half, W), "s": (half, W), "a1": (3, q, W), "b1": (3, q, W), "p": (2 * q, W),
        "a2": (3, e, W), "b2": (3, e, W), "c": (2 * e, W), "z": (7, 16, W), "fin": (rows, W),
    }


def shards(inputs, gain_in, conv_in, gain_mid, conv_mid, conv_skip, scored_grads, scored_frames):
    count = scored_frames.shape[1] * inputs.shape[0] * lax.axis_size("dp")
    scale = 1.0 / math.sqrt(count * RW * HT * W)
    vmem = pl.BlockSpec(memory_space=pltpu.VMEM)
    anyw = pl.BlockSpec(memory_space=pl.ANY)
    smem = pl.BlockSpec(memory_space=pltpu.SMEM)
    big, small = reduce_scratch(ROWS_IN), reduce_scratch(ROWS_MID)

    def buf(shape, dtype=BF16):
        return pltpu.VMEM(shape, dtype)

    scratch = [
        buf((6, 4, CI, W)), buf((6, 4, CI, W)), buf((SC * TM, RW, CO, W)), buf((6, 4, CO, W)),
        buf((6, 3 * CO, 4 * W)), buf((6, 4, CO, W)), buf((FR, 3 * CO, RW * W)),
        buf((FR, RW, CO, W)), buf((FR, RW, CO, W)),
        buf((3, 3, 3, CO, CI)), buf((3, 3, 3, CO, CO)), buf((27, CI, CO)), buf((27, CO, CO)),
    ]
    for name in ("g", "rc", "s"):
        scratch += [buf(big[name]), buf(small[name])]
    scratch += [buf(big["a1"]), buf(big["b1"]), buf(small["a1"]), buf(small["b1"])]
    scratch += [buf(big["p"]), buf(small["p"])]
    scratch += [buf(big["a2"]), buf(big["b2"]), buf(small["a2"]), buf(small["b2"])]
    for name in ("c", "z", "fin"):
        scratch += [buf(big[name]), buf(small[name])]
    scratch += [
        pltpu.SemaphoreType.DMA((N_SEMS,)), pltpu.SemaphoreType.DMA((N_SEMS,)),
        pltpu.SemaphoreType.DMA((N_LOCAL,)),
    ]

    def body(*refs):
        kernel(scale, *refs)

    grad_inputs, grad_in, grad_mid, grad_skip = pl.pallas_call(
        body,
        out_shape=(
            jax.ShapeDtypeStruct(inputs.shape, BF16),
            jax.ShapeDtypeStruct(conv_in.shape, F32),
            jax.ShapeDtypeStruct((27 * CO, CO), F32),
            jax.ShapeDtypeStruct(conv_skip.shape, F32),
        ),
        in_specs=[smem, anyw, vmem, anyw, vmem, anyw, vmem, anyw],
        out_specs=(vmem, vmem, vmem, vmem),
        scratch_shapes=scratch,
        compiler_params=pltpu.CompilerParams(
            collective_id=0, has_side_effects=True, vmem_limit_bytes=48 * 1024 * 1024
        ),
        name="block_backward",
    )(scored_frames, inputs, gain_in[None, :], conv_in, gain_mid[None, :], conv_mid, conv_skip, scored_grads)
    return grad_inputs, grad_in, grad_mid.reshape(conv_mid.shape), grad_skip


def solution(mesh):
    in_specs = (
        P("dp", "tm", "height", None, None),
        P(),
        P(),
        P(),
        P(),
        P(),
        P("dp", "tm", "height", None, None),
        P("dp", None),
    )
    out_specs = (P("dp", "tm", "height", None, None), P(), P(), P())
    return jax.shard_map(shards, mesh=mesh, in_specs=in_specs, out_specs=out_specs, check_vma=False)
```

time: 433 us -> 99.9 us (0.23)
  waiting for transfers between devices: 284 us -> 0 us
  Pallas kernels: 0 us -> 85.9 us
  starting transfers between devices: 36.6 us -> 0 us
  blocking collectives: 26.1 us -> 0 us
  matrix products: 24.6 us -> 0 us
  other arithmetic: 21 us -> 0 us
  between operations: 15.1 us -> 0.66 us
  local copies, waits for them, and re-layouts: 23.4 us -> 13.1 us
    psum x1 -> x0, waiting for transfers between devices: 284 us -> none  [shards(): lax.psum((grad_first, grad_mid, grad_skip), ('dp', 'tm', 'height'))]
    pallas_call x0 -> x1, Pallas kernels: none -> 85.9 us  [shards(): pl.pallas_call(body, out_shape=(jax.ShapeDtypeStruct(inputs.shape, BF16),...]
    ppermute x12 -> x0, starting transfers between devices: 36.6 us -> none  [the longest x4 21.6 us: with_halo(): lax.ppermute(tail, axis, [(i, (i + 1) % count) for i in range(ends)])]
    all_gather x1 -> x0, blocking collectives: 26.1 us -> none  [shards(): lax.all_gather(scored_grads, 'tm', axis=1, tiled=True)[0]]
    dot_general x48 -> x0, matrix products: 24.6 us -> none  [the longest x18 11 us: taps_input(): jnp.einsum('mc,fhmw->fhcw', matrix, window, preferred_element_type=jnp.fl...]
    concatenate x11 -> x0, other arithmetic: 16.3 us -> none  [the longest x4 9.08 us: shifted_stack(): return jnp.concatenate([padded[..., k:k + cols] for k in offsets], axis=2)]
    slice x11 -> x0, local copies, waits for them, and re-layouts: 8.1 us -> none  [the longest x4 2.35 us: extend_field(): piece = field[:depth] if ahead else field[count - depth:]]
    unnamed x87 -> x20, local copies, waits for them, and re-layouts: 8.38 us -> 13.1 us
  transfers between devices with their start and end apart: 13 -> 0, of which waited for: 1 -> 0; matrix products, arithmetic and copies ran while one was open for 8% -> 0% of each run, Pallas kernels for 0% -> 0%
where the time goes in v1:
time: 99.9 us; the launch traced here: 99.6 us
  Pallas kernels  85.9 us (86%)
  local copies, waits for them, and re-layouts  13.1 us (13%)
    pallas_call x1, Pallas kernels, shards(): pl.pallas_call(body, out_shape=(jax.ShapeDtypeStruct(inputs.shape, BF16),...  85.9 us
    unnamed x20, local copies, waits for them, and re-layouts  13.1 us

profile of v1, /device:TPU:1, one launch (start us, length us, event | category | flops | bytes accessed | tf_op | source)
XLA Modules:
  0.0 99.6 jit_solution(8076572768326888588)
XLA Ops:
  0.6 0.0 copy-start
  0.6 1.3 %copy-done = bf16[3,3,3,96,192]{4,3,2,1,0:T(8,128)(2,1)S(1)} copy-done((bf16[3,3,3,96,192]{4,3,2,1,0:T(8,128)(2,1)S(1)}, bf16[3,3,3,96,192]{4,3,2,1,0:T(8,128)(2,1)}, u32[]{:S(2)}) %copy-start) | copy-done | bytes 995352
  2.0 0.0 copy-start.1
  2.0 1.1 %copy-done.1 = bf16[3,3,3,96,96]{4,3,2,1,0:T(8,128)(2,1)S(1)} copy-done((bf16[3,3,3,96,96]{4,3,2,1,0:T(8,128)(2,1)S(1)}, bf16[3,3,3,96,96]{4,3,2,1,0:T(8,128)(2,1)}, u32[]{:S(2)}) %copy-start.1) | copy-done | bytes 497688
  3.0 0.0 copy-start.2
  3.0 1.0 copy-done.2
  4.0 0.0 copy-start.3
  4.0 0.9 copy-done.3
  4.9 0.0 copy-start.4
  4.9 0.8 copy-done.4
  5.7 0.0 copy-start.5
  5.7 0.7 copy-done.5
  6.4 0.0 copy-start.6
  6.4 0.7 copy-done.6
  7.1 0.0 copy-start.7
  7.1 0.7 copy-done.7
  7.7 85.9 %block_backward.1 = (bf16[1,4,2,192,128]{4,3,2,1,0:T(8,128)(2,1)S(1)}, f32[3,3,3,96,192]{4,3,2,1,0:T(8,128)}, f32[2592,96]{1,0:T(8,128)S(1)}, f32[96,192]{1,0:T(8,128)S(1)}) custom-call(s32[1,16]{1,0:T(1,128)S(1)} %copy-done.6, bf16[1,4,2,192,128]{4,3,2,1,0:T(8,128)(2,1)S(1)} %copy-done.2, f32[1,192]{1,0:T(1,128)S(1)} %bitcast.4, ...), custom_call_target="tpu_custom_call" | custom-call | tf_op jit(solution)/shard_map/block_backward/pallas_call | solution.py:580
  93.6 0.7 copy.16
  94.3 3.5 %copy.17 = f32[3,3,3,96,192]{4,3,2,1,0:T(8,128)} copy(f32[3,3,3,96,192]{4,3,2,1,0:T(8,128)} %get-tuple-element.17) | data formatting | bytes 3981312
  97.9 1.1 %copy.18 = f32[3,3,3,96,96]{4,3,2,1,0:T(8,128)} copy(f32[3,3,3,96,96]{4,3,2,1,0:T(8,128)S(1)} %bitcast.3) | data formatting | bytes 1990656
  98.9 0.6 copy.19
Async XLA Ops:
  0.6 1.3 %copy-start = (bf16[3,3,3,96,192]{4,3,2,1,0:T(8,128)(2,1)S(1)}, bf16[3,3,3,96,192]{4,3,2,1,0:T(8,128)(2,1)}, u32[]{:S(2)}) copy-start(bf16[3,3,3,96,192]{4,3,2,1,0:T(8,128)(2,1)} %refs_3_.1) | copy-start | bytes 2985988
  2.0 1.1 %copy-start.1 = (bf16[3,3,3,96,96]{4,3,2,1,0:T(8,128)(2,1)S(1)}, bf16[3,3,3,96,96]{4,3,2,1,0:T(8,128)(2,1)}, u32[]{:S(2)}) copy-start(bf16[3,3,3,96,96]{4,3,2,1,0:T(8,128)(2,1)} %refs_5_.1) | copy-start | bytes 1492996
  3.0 1.0 copy-start.2
  4.0 0.9 copy-start.3
  4.9 0.8 copy-start.4
  5.7 0.7 copy-start.5
  6.4 0.7 copy-start.6
  7.1 0.7 copy-start.7

commit v2 on v1

--- a/solution.py
+++ b/solution.py
@@ -79,8 +79,8 @@
         return list(range(at, at + count))
 
 
-N_SEMS = 120
-N_LOCAL = 8
+N_SEMS = 192
+N_LOCAL = 24
 
 
 def when(cond, fn):
@@ -91,8 +91,8 @@
 
 
 def kernel(scale, sf, x_hbm, gain_in, win_hbm, gain_mid, wmid_hbm, wskip, sg_hbm,
-           out_x, out_in, out_mid, out_skip,
-           XE, H1, SG, CE, CS, GE, GS, A1, H2, WIN, WMID, WTI, WTM,
+           out_x, out_in, out_mid,
+           OX,           XE, H1, SG, CE, CS, GE, GS, A1, H2, WIN, WMID, WTI, WTM,
            g_in, g_mid, rc_in, rc_mid, s_in, s_mid,
            a1_in, b1_in, a1_mid, b1_mid, p_in, p_mid, a2_in, b2_in, a2_mid, b2_mid,
            c_in, c_mid, z_in, z_mid, fin_in, fin_mid,
@@ -122,6 +122,13 @@
     def z_peer(v):
         return dev(hh=v * 2 + x_hi)
 
+    kept = []
+
+    def keep(src, dst):
+        copy = pltpu.make_async_copy(src, dst, local.at[4 + len(kept)])
+        copy.start()
+        kept.append(copy)
+
     class Copy:
         def __init__(self, src, dst, to, s_if=None, r_if=None):
             i = sems.take(1)[0]
@@ -150,7 +157,8 @@
         item.start()
 
     barrier = pltpu.get_barrier_semaphore()
-    friends = [dev(tt=(t + k) % TM) for k in range(1, TM)]
+    friends = [y_peer((y + k) % 4) for k in (1, 2, 3)]
+    friends += [dev(tt=(t + k) % TM) for k in (1, 7, 4)]
     friends += [dev(hh=(h + k) % HT) for k in (1, 15, 2, 4, 6, 8, 10, 12, 14)]
     friends += [dev(tt=(t + a) % TM, hh=(h + b) % HT) for a in (1, 7) for b in (1, 15)]
     friends += [x_peer(3 - xx), dev(cc=1 - c)]
@@ -185,10 +193,10 @@
     has_n, has_p = h < HT - 1, h > 0
     t_n, t_p = t < TM - 1, t > 0
 
-    gather = [
-        Copy(sg_hbm.at[0], SG.at[pl.ds(SC * t, SC)], dev(tt=(t + k) % TM)) for k in (1, 7, 2, 6, 3, 5, 4)
-    ]
-    for item in gather:
+    other_t = (t + TM // 2) % TM
+    across = [Copy(sg_hbm.at[0, j], SG.at[SC * t + j], dev(tt=other_t)) for j in range(SC)]
+    along = [Copy(sg_hbm.at[0], SG.at[pl.ds(SC * t, SC)], y_peer((y + k) % 4)) for k in (1, 3, 2)]
+    for item in across + along:
         item.start()
 
     src = x_hbm.at[0]
@@ -201,7 +209,17 @@
         Copy(src.at[pl.ds(2, 2), 0], XE.at[pl.ds(0, 2), 3], dev(tt=t + 1, hh=h - 1),
              both(t_n, has_p), both(t_p, has_n)),
     ]
-    for item in x_halo:
+    for item in x_halo[:2]:
+        item.start()
+
+    for j in range(SC):
+        across[j].got()
+        at_j = SC * other_t + j
+        onward = [Copy(SG.at[at_j], SG.at[at_j], y_peer((y + k) % 4)) for k in (1, 3, 2)]
+        for item in onward:
+            item.start()
+        along += onward
+    for item in x_halo[2:]:
         item.start()
 
     g1 = column(gain_in[...], CI)
@@ -229,7 +247,7 @@
     lax.fori_loop(0, 8, h1_own, 0)
 
     loc[1].wait()
-    for item in gather:
+    for item in along:
         item.got()
     for f in range(6):
         frame = t * FR + f
@@ -337,7 +355,7 @@
     for j in range(2):
         g_in[pl.ds(3456 + 288 * j, 288)] = acc[:, j * W:(j + 1) * W].astype(BF16)
 
-    def reduce(g, rc, s, a1, b1, p, a2, b2, cc, zz, fin, rows):
+    def reduce(g, rc, s, a1, b1, p, a2, b2, cc, zz, fin, out, rows):
         half = rows // 2
         ha = half // 2
         q = ha // 4
@@ -355,33 +373,40 @@
                 out = out + term.astype(F32)
             return out.astype(BF16)
 
-        step = 128
-
-        core = Copy(g.at[pl.ds(other, half)], rc, dev(cc=1 - c))
-        core.start()
-        yield
-        core.got()
-
-        def add_core(i, _):
-            o = pl.multiple_of(i * step, step)
-            s[pl.ds(o, step)] = total([g[pl.ds(pl.multiple_of(mine + o, step), step)], rc[pl.ds(o, step)]])
-            return 0
-
-        lax.fori_loop(0, half // step, add_core, 0)
+        near = (1, 3, 2)
+        far = (2, 1, 3, 0)
+
+        def piece_a(base, k):
+            return at(base + (xx + 4 - k) % 4 * q, q)
+
+        def piece_b(base, k):
+            return at(base + ha + (y + 4 - k) % 4 * q, q)
+
+        core = []
+        for k in far:
+            for piece in (piece_a, piece_b):
+                core.append(Copy(g.at[piece(other, k)], rc.at[piece(0, k)], dev(cc=1 - c)))
+                core[-1].start()
+        yield
         one = []
-        for k in (1, 3, 2):
-            xp, yp = (xx + k) % 4, (y + k) % 4
-            one.append(Copy(s.at[at(xp * q, q)], a1.at[k - 1], x_peer(xp)))
-            one.append(Copy(s.at[at(ha + yp * q, q)], b1.at[k - 1], y_peer(yp)))
-        for item in one:
-            item.start()
+        for k in far[:3]:
+            for n, piece in enumerate((piece_a, piece_b)):
+                core.pop(0).got()
+                s[piece(0, k)] = total([g[piece(mine, k)], rc[piece(0, k)]])
+                if n == 0:
+                    one.append(Copy(s.at[piece(0, k)], a1.at[k - 1], x_peer((xx + 4 - k) % 4)))
+                else:
+                    one.append(Copy(s.at[piece(0, k)], b1.at[k - 1], y_peer((y + 4 - k) % 4)))
+                one[-1].start()
+        for item in core:
+            item.got()
         yield
         for item in one:
             item.got()
-        p[pl.ds(0, q)] = total([s[at(xx * q, q)], a1[0], a1[1], a1[2]])
-        p[pl.ds(q, q)] = total([s[at(ha + y * q, q)], b1[0], b1[1], b1[2]])
+        p[pl.ds(0, q)] = total([g[piece_a(mine, 0)], rc[piece_a(0, 0)], a1[0], a1[1], a1[2]])
+        p[pl.ds(q, q)] = total([g[piece_b(mine, 0)], rc[piece_b(0, 0)], b1[0], b1[1], b1[2]])
         two = []
-        for k in (1, 3, 2):
+        for k in (2, 1, 3):
             xp, yp = (xx + k) % 4, (y + k) % 4
             two.append(Copy(p.at[at(yp * e, e)], a2.at[k - 1], y_peer(yp)))
             two.append(Copy(p.at[at(q + xp * e, e)], b2.at[k - 1], x_peer(xp)))
@@ -392,7 +417,7 @@
             item.got()
         cc[pl.ds(0, e)] = total([p[at(y * e, e)], a2[0], a2[1], a2[2]])
         cc[pl.ds(e, e)] = total([p[at(q + xx * e, e)], b2[0], b2[1], b2[2]])
-        ks = (1, 7, 2, 6, 3, 5, 4)
+        ks = (4, 3, 5, 2, 6, 1, 7)
         own = None if owners == 8 else z < owners
         three = []
         for k in ks:
@@ -424,34 +449,56 @@
         yield
         for item in four:
             item.got()
-        five = []
-        for k in (1, 3, 2):
-            xp, yp = (xx + k) % 4, (y + k) % 4
-            five.append(Copy(fin.at[at(base_a, e)], fin.at[at(base_a, e)], y_peer(yp)))
-            five.append(Copy(fin.at[at(base_b, e)], fin.at[at(base_b, e)], x_peer(xp)))
-        for item in five:
-            item.start()
-        yield
-        for item in five:
+        def part_a(k):
+            return at(mine + xx * q + (y + 4 - k) % 4 * e, e)
+
+        def part_b(k):
+            return at(mine + ha + y * q + (xx + 4 - k) % 4 * e, e)
+
+        six = {k: [] for k in near}
+
+        def onward(k):
+            for m in (2, 1, 3):
+                six[m].append((Copy(fin.at[part_a(k)], fin.at[part_a(k)], x_peer((xx + m) % 4)),
+                               Copy(fin.at[part_b(k)], fin.at[part_b(k)], y_peer((y + m) % 4))))
+                for item in six[m][-1]:
+                    item.start()
+
+        five = {}
+        for k in (2, 1, 3):
+            five[k] = (Copy(fin.at[part_a(0)], fin.at[part_a(0)], y_peer((y + k) % 4)),
+                       Copy(fin.at[part_b(0)], fin.at[part_b(0)], x_peer((xx + k) % 4)))
+            for item in five[k]:
+                item.start()
+        onward(0)
+        yield
+        for k in near:
+            for item in five[k]:
+                item.got()
+            onward(k)
+        last = []
+
+        def deliver(k):
+            for piece in (piece_a, piece_b):
+                rng = piece(mine, k)
+                last.append(Copy(fin.at[rng], out.at[rng], dev(cc=1 - c)))
+                last[-1].start()
+                keep(fin.at[rng], out.at[rng])
+
+        deliver(0)
+        yield
+        for m in near:
+            for items in six[m]:
+                for item in items:
+                    item.got()
+            deliver(m)
+        yield
+        for item in last:
             item.got()
-        six = []
-        for k in (1, 3, 2):
-            xp, yp = (xx + k) % 4, (y + k) % 4
-            six.append(Copy(fin.at[at(mine + xx * q, q)], fin.at[at(mine + xx * q, q)], x_peer(xp)))
-            six.append(Copy(fin.at[at(mine + ha + y * q, q)], fin.at[at(mine + ha + y * q, q)], y_peer(yp)))
-        for item in six:
-            item.start()
-        yield
-        for item in six:
-            item.got()
-        last = Copy(fin.at[pl.ds(mine, half)], fin.at[pl.ds(mine, half)], dev(cc=1 - c))
-        last.start()
-        yield
-        last.got()
-        yield
-
-    big = reduce(g_in, rc_in, s_in, a1_in, b1_in, p_in, a2_in, b2_in, c_in, z_in, fin_in, ROWS_IN)
-    small = reduce(g_mid, rc_mid, s_mid, a1_mid, b1_mid, p_mid, a2_mid, b2_mid, c_mid, z_mid, fin_mid, ROWS_MID)
+        yield
+
+    big = reduce(g_in, rc_in, s_in, a1_in, b1_in, p_in, a2_in, b2_in, c_in, z_in, fin_in, out_in, ROWS_IN)
+    small = reduce(g_mid, rc_mid, s_mid, a1_mid, b1_mid, p_mid, a2_mid, b2_mid, c_mid, z_mid, fin_mid, out_mid, ROWS_MID)
     next(big)
 
     def cot_shift(f, _):
@@ -498,7 +545,7 @@
             part = acc[:, r * W:(r + 1) * W]
             gh1 = part[CI:2 * CI] + ahead(part[:CI]) + behind(part[2 * CI:])
             grad = norm_pull(XE[2 + f, 1 + r].astype(F32), g1, gh1) + skip[:, r * W:(r + 1) * W]
-            out_x[0, f, r] = grad.astype(BF16)
+            OX[f, r] = grad.astype(BF16)
 
     for item in ga_halo:
         item.got()
@@ -506,34 +553,53 @@
         back_in(f)
         next(big)
         next(small)
-    for _ in range(2):
+    keep(OX, out_x.at[0])
+    for _ in range(3):
         next(big)
         next(small)
-    next(big)
-
+    for item in sent:
+        item.left()
+    for item in kept:
+        item.wait()
+
+
+def assemble(scale, gx, fi, fm, out_x, out_in, out_mid, out_skip, BI, BM, BS, sem):
+    copies = []
+
+    def put(src, dst):
+        copy = pltpu.make_async_copy(src, dst, sem.at[len(copies)])
+        copy.start()
+        copies.append(copy)
+
+    put(gx, out_x)
     for n, taps in enumerate(PAIRS):
         for kw in range(3):
-            low = fin_in[pl.ds(864 * n + 576 + CO * kw, CO)].astype(F32) * scale
+            low = fi[pl.ds(864 * n + 576 + CO * kw, CO)].astype(F32) * scale
             for j, i in enumerate(taps):
                 kt, kh = TAPS[i]
-                high = fin_in[pl.ds(864 * n + 288 * j + CO * kw, CO)].astype(F32) * scale
-                out_in[kt, kh, kw, :, pl.ds(0, W)] = high
+                BI[kt, kh, kw, :, pl.ds(0, W)] = fi[pl.ds(864 * n + 288 * j + CO * kw, CO)].astype(F32) * scale
                 rest = low if j == 0 else pltpu.roll(low, 64, 1)
-                out_in[kt, kh, kw, :, pl.ds(W, 64)] = rest[:, :64]
+                BI[kt, kh, kw, :, pl.ds(W, 64)] = rest[:, :64]
+        for i in taps:
+            put(BI.at[TAPS[i]], out_in.at[TAPS[i]])
     for kw in range(3):
-        out_in[2, 2, kw, :, pl.ds(0, W)] = fin_in[pl.ds(3456 + CO * kw, CO)].astype(F32) * scale
-        out_in[2, 2, kw, :, pl.ds(W, 64)] = (fin_in[pl.ds(3744 + CO * kw, CO)].astype(F32) * scale)[:, :64]
-    out_skip[pl.ds(32, 64), pl.ds(0, W)] = fin_in[pl.ds(4032, 64)].astype(F32) * scale
-    next(small)
+        BI[2, 2, kw, :, pl.ds(0, W)] = fi[pl.ds(3456 + CO * kw, CO)].astype(F32) * scale
+        BI[2, 2, kw, :, pl.ds(W, 64)] = (fi[pl.ds(3744 + CO * kw, CO)].astype(F32) * scale)[:, :64]
+    put(BI.at[2, 2], out_in.at[2, 2])
+    tail = fm[pl.ds(1920, CO)].astype(F32) * scale
+    BS[pl.ds(0, 32), pl.ds(0, W)] = fm[pl.ds(2016, 32)].astype(F32) * scale
+    BS[pl.ds(32, 64), pl.ds(0, W)] = fi[pl.ds(4032, 64)].astype(F32) * scale
+    BS[:, pl.ds(W, 64)] = pltpu.roll(tail, 64, 1)[:, :64]
+    put(BS, out_skip)
     for j in range(20):
-        out_mid[pl.ds(W * j, W)] = (fin_mid[pl.ds(CO * j, CO)].astype(F32) * scale).T
-    tail = fin_mid[pl.ds(1920, CO)].astype(F32) * scale
-    out_mid[pl.ds(2560, 32)] = tail.T[:32]
-    out_skip[:, pl.ds(W, 64)] = pltpu.roll(tail, 64, 1)[:, :64]
-    out_skip[pl.ds(0, 32), pl.ds(0, W)] = fin_mid[pl.ds(2016, 32)].astype(F32) * scale
-
-    for item in sent:
-        item.left()
+        BM[pl.ds(W * j, W)] = (fm[pl.ds(CO * j, CO)].astype(F32) * scale).T
+        if j % 5 == 4:
+            rows = pl.ds(W * (j - 4), 5 * W)
+            put(BM.at[rows], out_mid.at[rows])
+    BM[pl.ds(2560, 32)] = tail.T[:32]
+    put(BM.at[pl.ds(2560, 32)], out_mid.at[pl.ds(2560, 32)])
+    for copy in copies:
+        copy.wait()
 
 
 def reduce_scratch(rows):
@@ -557,6 +623,7 @@
         return pltpu.VMEM(shape, dtype)
 
     scratch = [
+        buf((FR, RW, CI, W)),
         buf((6, 4, CI, W)), buf((6, 4, CI, W)), buf((SC * TM, RW, CO, W)), buf((6, 4, CO, W)),
         buf((6, 3 * CO, 4 * W)), buf((6, 4, CO, W)), buf((FR, 3 * CO, RW * W)),
         buf((FR, RW, CO, W)), buf((FR, RW, CO, W)),
@@ -577,22 +644,42 @@
     def body(*refs):
         kernel(scale, *refs)
 
+    grad_x, sum_in, sum_mid = pl.pallas_call(
+        body,
+        out_shape=(
+            jax.ShapeDtypeStruct(inputs.shape, BF16),
+            jax.ShapeDtypeStruct((ROWS_IN, W), BF16),
+            jax.ShapeDtypeStruct((ROWS_MID, W), BF16),
+        ),
+        in_specs=[smem, anyw, vmem, anyw, vmem, anyw, vmem, anyw],
+        out_specs=(anyw, anyw, anyw),
+        scratch_shapes=scratch,
+        compiler_params=pltpu.CompilerParams(
+            collective_id=0, has_side_effects=True, vmem_limit_bytes=63 * 1024 * 1024
+        ),
+        name="block_backward",
+    )(scored_frames, inputs, gain_in[None, :], conv_in, gain_mid[None, :], conv_mid, conv_skip, scored_grads)
+
+    def last(*refs):
+        assemble(scale, *refs)
+
     grad_inputs, grad_in, grad_mid, grad_skip = pl.pallas_call(
-        body,
+        last,
         out_shape=(
             jax.ShapeDtypeStruct(inputs.shape, BF16),
             jax.ShapeDtypeStruct(conv_in.shape, F32),
             jax.ShapeDtypeStruct((27 * CO, CO), F32),
             jax.ShapeDtypeStruct(conv_skip.shape, F32),
         ),
-        in_specs=[smem, anyw, vmem, anyw, vmem, anyw, vmem, anyw],
-        out_specs=(vmem, vmem, vmem, vmem),
-        scratch_shapes=scratch,
-        compiler_params=pltpu.CompilerParams(
-            collective_id=0, has_side_effects=True, vmem_limit_bytes=48 * 1024 * 1024
-        ),
-        name="block_backward",
-    )(scored_frames, inputs, gain_in[None, :], conv_in, gain_mid[None, :], conv_mid, conv_skip, scored_grads)
+        in_specs=[vmem, vmem, vmem],
+        out_specs=(anyw, anyw, anyw, anyw),
+        scratch_shapes=[
+            buf(conv_in.shape, F32), buf((27 * CO, CO), F32), buf(conv_skip.shape, F32),
+            pltpu.SemaphoreType.DMA((16,)),
+        ],
+        compiler_params=pltpu.CompilerParams(vmem_limit_bytes=63 * 1024 * 1024),
+        name="assemble",
+    )(grad_x, sum_in, sum_mid)
     return grad_inputs, grad_in, grad_mid.reshape(conv_mid.shape), grad_skip
 
 

time: 99.9 us -> 84.4 us (0.84)
  local copies, waits for them, and re-layouts: 13.1 us -> 0 us
  Pallas kernels: 85.9 us -> 83.6 us
    unnamed x20 -> x0, local copies, waits for them, and re-layouts: 13.1 us -> none
    pallas_call x1, Pallas kernels: 85.9 us -> 79.9 us  [shards(): pl.pallas_call(body, out_shape=(jax.ShapeDtypeStruct(inputs.shape, BF16),...]
    pallas_call x0 -> x1, Pallas kernels: none -> 3.7 us  [shards(): pl.pallas_call(last, out_shape=(jax.ShapeDtypeStruct(inputs.shape, BF16),...]
where the time goes in v2:
time: 84.4 us; the launch traced here: 84.2 us
  Pallas kernels  83.6 us (99%)
    pallas_call x1, Pallas kernels, shards(): pl.pallas_call(body, out_shape=(jax.ShapeDtypeStruct(inputs.shape, BF16),...  79.9 us
    pallas_call x1, Pallas kernels, shards(): pl.pallas_call(last, out_shape=(jax.ShapeDtypeStruct(inputs.shape, BF16),...  3.7 us

profile of v2, /device:TPU:1, one launch (start us, length us, event | category | flops | bytes accessed | tf_op | source)
XLA Modules:
  0.0 84.2 jit_solution(5082711869609564136)
XLA Ops:
  0.6 79.9 %block_backward.1 = (bf16[1,4,2,192,128]{4,3,2,1,0:T(8,128)(2,1)}, bf16[4096,128]{1,0:T(8,128)(2,1)}, bf16[2048,128]{1,0:T(8,128)(2,1)}) custom-call(s32[1,16]{1,0:T(1,128)} %refs_0_.1, bf16[1,4,2,192,128]{4,3,2,1,0:T(8,128)(2,1)} %refs_1_.1, f32[1,192]{1,0:T(1,128)} %bitcast.3, bf16[3,3,3,96,192]{4,3,2,1,0:T(8,128)(2,1)} %refs_3_.1, f32[1,96]{1,0:T(1,128)} %bitcast.4, ...), custom_call_target="tpu_custom_call" | custom-call | tf_op jit(solution)/shard_map/block_backward/pallas_call | solution.py:647
  80.5 3.7 %assemble.1 = (bf16[1,4,2,192,128]{4,3,2,1,0:T(8,128)(2,1)}, f32[3,3,3,96,192]{4,3,2,1,0:T(8,128)}, f32[2592,96]{1,0:T(8,128)}, f32[96,192]{1,0:T(8,128)}) custom-call(bf16[1,4,2,192,128]{4,3,2,1,0:T(8,128)(2,1)} %get-tuple-element.11.refs_0_, bf16[4096,128]{1,0:T(8,128)(2,1)} %get-tuple-element.12.refs_1_, bf16[2048,128]{1,0:T(8,128)(2,1)} %get-tuple-element.13.refs_2_), custom_call_target="tpu_custom_call" | custom-call | tf_op jit(solution)/shard_map/assemble/pallas_call | solution.py:666

commit v3 on v2

--- a/solution.py
+++ b/solution.py
@@ -92,7 +92,7 @@
 
 def kernel(scale, sf, x_hbm, gain_in, win_hbm, gain_mid, wmid_hbm, wskip, sg_hbm,
            out_x, out_in, out_mid,
-           OX,           XE, H1, SG, CE, CS, GE, GS, A1, H2, WIN, WMID, WTI, WTM,
+           OX,           XE, H1, SG, CE, CS, GE, GS, ACC, A1, H2, WIN, WMID, WTI, WTM,
            g_in, g_mid, rc_in, rc_mid, s_in, s_mid,
            a1_in, b1_in, a1_mid, b1_mid, p_in, p_mid, a2_in, b2_in, a2_mid, b2_mid,
            c_in, c_mid, z_in, z_mid, fin_in, fin_mid,
@@ -157,10 +157,10 @@
         item.start()
 
     barrier = pltpu.get_barrier_semaphore()
-    friends = [y_peer((y + k) % 4) for k in (1, 2, 3)]
+    friends = [dev(hh=(h + k) % HT) for k in (8, 6, 10, 4, 12, 2, 14, 1, 15)]
+    friends += [dev(tt=(t + a) % TM, hh=(h + b) % HT) for a in (1, 7) for b in (1, 15)]
+    friends += [y_peer((y + k) % 4) for k in (1, 2, 3)]
     friends += [dev(tt=(t + k) % TM) for k in (1, 7, 4)]
-    friends += [dev(hh=(h + k) % HT) for k in (1, 15, 2, 4, 6, 8, 10, 12, 14)]
-    friends += [dev(tt=(t + a) % TM, hh=(h + b) % HT) for a in (1, 7) for b in (1, 15)]
     friends += [x_peer(3 - xx), dev(cc=1 - c)]
     for to in friends:
         pl.semaphore_signal(barrier, inc=1, device_id=to, device_id_type=MESH)
@@ -275,7 +275,24 @@
         skip_a = skip_a + dot_nt(cot, xs[:W])
         skip_b = skip_b + dot_nt(cot, jnp.concatenate([jnp.zeros((64, 2 * W), BF16), xs[W:]], axis=0))
     g_mid[pl.ds(2016, 32)] = skip_a[:32].astype(BF16)
-    g_in[pl.ds(4032, 64)] = skip_a[32:].astype(BF16)
+    g_in[pl.ds(2016, 32)] = skip_a[32:64].astype(BF16)
+    g_in[pl.ds(4064, 32)] = skip_a[64:].astype(BF16)
+
+    def mid_part(g, r, khs):
+        acc = jnp.zeros((3 * CO, 2 * W), F32)
+        for kt in range(3):
+            for kh in khs:
+                f, row = 2 * g + 2 - kt, r + 2 - kh
+                matrix = WTM[pl.ds(9 * kt + 3 * kh, 3)].reshape(3 * CO, CO)
+                acc = acc + dot(matrix, jnp.concatenate([CE[f, row], CE[f + 1, row]], axis=1))
+        return acc
+
+    def own_mid(g, _):
+        ACC[g, 0] = mid_part(g, 0, (0, 1))
+        ACC[g, 1] = mid_part(g, 1, (1, 2))
+        return 0
+
+    lax.fori_loop(0, 2, own_mid, 0)
 
     for item in x_halo:
         item.got()
@@ -310,23 +327,23 @@
     for item in cot_halo:
         item.got()
 
-    def back_mid(f, _):
-        acc = jnp.zeros((3 * CO, 2 * W), F32)
-        for n, (kt, kh) in enumerate(TAPS):
-            acc = acc + dot(WTM[pl.ds(3 * n, 3)].reshape(3 * CO, CO), pair(CE, f + 2 - kt, 2 - kh))
+    def back_mid(g, _):
         for r in range(RW):
-            part = acc[:, r * W:(r + 1) * W]
-            gh2 = part[CO:2 * CO] + ahead(part[:CO]) + behind(part[2 * CO:])
-            ga1 = norm_pull(A1[f, r].astype(F32), g2, gh2).astype(BF16)
-            GE[f, 1 + r] = ga1
-            wide = ga1.astype(F32)
-            lanes = pl.ds(r * W, W)
-            GS[f, pl.ds(0, CO), lanes] = ahead(wide).astype(BF16)
-            GS[f, pl.ds(CO, CO), lanes] = ga1
-            GS[f, pl.ds(2 * CO, CO), lanes] = behind(wide).astype(BF16)
+            acc = ACC[g, r] + mid_part(g, r, (2,) if r == 0 else (0,))
+            for j in range(2):
+                f = 2 * g + j
+                part = acc[:, j * W:(j + 1) * W]
+                gh2 = part[CO:2 * CO] + ahead(part[:CO]) + behind(part[2 * CO:])
+                ga1 = norm_pull(A1[f, r].astype(F32), g2, gh2).astype(BF16)
+                GE[f, 1 + r] = ga1
+                wide = ga1.astype(F32)
+                lanes = pl.ds(r * W, W)
+                GS[f, pl.ds(0, CO), lanes] = ahead(wide).astype(BF16)
+                GS[f, pl.ds(CO, CO), lanes] = ga1
+                GS[f, pl.ds(2 * CO, CO), lanes] = behind(wide).astype(BF16)
         return 0
 
-    lax.fori_loop(0, FR, back_mid, 0)
+    lax.fori_loop(0, 2, back_mid, 0)
     ga_halo = [
         Copy(GE.at[pl.ds(0, 4), 2], GE.at[pl.ds(0, 4), 0], dev(hh=h + 1), has_n, has_p),
         Copy(GE.at[pl.ds(0, 4), 1], GE.at[pl.ds(0, 4), 3], dev(hh=h - 1), has_p, has_n),
@@ -339,23 +356,7 @@
     for item in ga_halo:
         item.start()
 
-    for n, taps in enumerate(PAIRS):
-        acc = jnp.zeros((3 * CO, 3 * W), F32)
-        for f in range(FR):
-            one = [pair(H1, f + TAPS[i][0], TAPS[i][1]) for i in taps]
-            rhs = jnp.concatenate([one[0][:W], one[1][:W], one[0][W:], one[1][W:]], axis=0)
-            acc = acc + dot_nt(GS[f], rhs)
-        for j in range(3):
-            g_in[pl.ds(864 * n + 288 * j, 288)] = acc[:, j * W:(j + 1) * W].astype(BF16)
-    acc = jnp.zeros((3 * CO, 2 * W), F32)
-    for f in range(FR):
-        one = pair(H1, f + 2, 2)
-        rhs = jnp.concatenate([one, jnp.zeros((64, 2 * W), BF16)], axis=0)
-        acc = acc + dot_nt(GS[f], rhs)
-    for j in range(2):
-        g_in[pl.ds(3456 + 288 * j, 288)] = acc[:, j * W:(j + 1) * W].astype(BF16)
-
-    def reduce(g, rc, s, a1, b1, p, a2, b2, cc, zz, fin, out, rows):
+    def reduce(g, rc, s, a1, b1, p, a2, b2, cc, zz, fin, out, rows, parts=None):
         half = rows // 2
         ha = half // 2
         q = ha // 4
@@ -383,15 +384,25 @@
             return at(base + ha + (y + 4 - k) % 4 * q, q)
 
         core = []
-        for k in far:
-            for piece in (piece_a, piece_b):
-                core.append(Copy(g.at[piece(other, k)], rc.at[piece(0, k)], dev(cc=1 - c)))
+        if parts:
+            for off, n in parts:
+                core.append(Copy(g.at[at(other + off, n)], rc.at[pl.ds(off, n)], dev(cc=1 - c)))
                 core[-1].start()
-        yield
+                yield
+            for item in core:
+                item.got()
+            core = []
+        else:
+            for k in far:
+                for piece in (piece_a, piece_b):
+                    core.append(Copy(g.at[piece(other, k)], rc.at[piece(0, k)], dev(cc=1 - c)))
+                    core[-1].start()
+            yield
         one = []
         for k in far[:3]:
             for n, piece in enumerate((piece_a, piece_b)):
-                core.pop(0).got()
+                if core:
+                    core.pop(0).got()
                 s[piece(0, k)] = total([g[piece(mine, k)], rc[piece(0, k)]])
                 if n == 0:
                     one.append(Copy(s.at[piece(0, k)], a1.at[k - 1], x_peer((xx + 4 - k) % 4)))
@@ -497,8 +508,27 @@
             item.got()
         yield
 
-    big = reduce(g_in, rc_in, s_in, a1_in, b1_in, p_in, a2_in, b2_in, c_in, z_in, fin_in, out_in, ROWS_IN)
+    big = reduce(g_in, rc_in, s_in, a1_in, b1_in, p_in, a2_in, b2_in, c_in, z_in, fin_in, out_in, ROWS_IN,
+                 [(432 * n, 432) for n in range(4)] + [(1728, 320)])
     small = reduce(g_mid, rc_mid, s_mid, a1_mid, b1_mid, p_mid, a2_mid, b2_mid, c_mid, z_mid, fin_mid, out_mid, ROWS_MID)
+    for n, taps in enumerate(PAIRS):
+        acc = jnp.zeros((3 * CO, 3 * W), F32)
+        for f in range(FR):
+            one = [pair(H1, f + TAPS[i][0], TAPS[i][1]) for i in taps]
+            rhs = jnp.concatenate([one[0][:W], one[1][:W], one[0][W:], one[1][W:]], axis=0)
+            acc = acc + dot_nt(GS[f], rhs)
+        blocks = [acc[:, j * W:(j + 1) * W].astype(BF16) for j in range(3)]
+        g_in[pl.ds(432 * n, 288)] = blocks[0]
+        g_in[pl.ds(432 * n + 288, 144)] = blocks[1][:144]
+        g_in[pl.ds(2048 + 432 * n, 144)] = blocks[1][144:]
+        g_in[pl.ds(2048 + 432 * n + 144, 288)] = blocks[2]
+        next(big)
+    acc = jnp.zeros((3 * CO, 2 * W), F32)
+    for f in range(FR):
+        rhs = jnp.concatenate([pair(H1, f + 2, 2), jnp.zeros((64, 2 * W), BF16)], axis=0)
+        acc = acc + dot_nt(GS[f], rhs)
+    for j in range(2):
+        g_in[pl.ds(2048 * j + 1728, 288)] = acc[:, j * W:(j + 1) * W].astype(BF16)
     next(big)
 
     def cot_shift(f, _):
@@ -571,24 +601,35 @@
         copy.start()
         copies.append(copy)
 
+    def rows(n, at, count):
+        if at + count <= 432:
+            value = fi[pl.ds(432 * n + at, count)]
+        elif at >= 432:
+            value = fi[pl.ds(2048 + 432 * n + at - 432, count)]
+        else:
+            cut = 432 - at
+            value = jnp.concatenate([fi[pl.ds(432 * n + at, cut)], fi[pl.ds(2048 + 432 * n, count - cut)]], axis=0)
+        return value.astype(F32) * scale
+
     put(gx, out_x)
     for n, taps in enumerate(PAIRS):
         for kw in range(3):
-            low = fi[pl.ds(864 * n + 576 + CO * kw, CO)].astype(F32) * scale
+            low = rows(n, 576 + CO * kw, CO)
             for j, i in enumerate(taps):
                 kt, kh = TAPS[i]
-                BI[kt, kh, kw, :, pl.ds(0, W)] = fi[pl.ds(864 * n + 288 * j + CO * kw, CO)].astype(F32) * scale
+                BI[kt, kh, kw, :, pl.ds(0, W)] = rows(n, 288 * j + CO * kw, CO)
                 rest = low if j == 0 else pltpu.roll(low, 64, 1)
                 BI[kt, kh, kw, :, pl.ds(W, 64)] = rest[:, :64]
         for i in taps:
             put(BI.at[TAPS[i]], out_in.at[TAPS[i]])
     for kw in range(3):
-        BI[2, 2, kw, :, pl.ds(0, W)] = fi[pl.ds(3456 + CO * kw, CO)].astype(F32) * scale
-        BI[2, 2, kw, :, pl.ds(W, 64)] = (fi[pl.ds(3744 + CO * kw, CO)].astype(F32) * scale)[:, :64]
+        BI[2, 2, kw, :, pl.ds(0, W)] = fi[pl.ds(1728 + CO * kw, CO)].astype(F32) * scale
+        BI[2, 2, kw, :, pl.ds(W, 64)] = (fi[pl.ds(3776 + CO * kw, CO)].astype(F32) * scale)[:, :64]
     put(BI.at[2, 2], out_in.at[2, 2])
     tail = fm[pl.ds(1920, CO)].astype(F32) * scale
     BS[pl.ds(0, 32), pl.ds(0, W)] = fm[pl.ds(2016, 32)].astype(F32) * scale
-    BS[pl.ds(32, 64), pl.ds(0, W)] = fi[pl.ds(4032, 64)].astype(F32) * scale
+    BS[pl.ds(32, 32), pl.ds(0, W)] = fi[pl.ds(2016, 32)].astype(F32) * scale
+    BS[pl.ds(64, 32), pl.ds(0, W)] = fi[pl.ds(4064, 32)].astype(F32) * scale
     BS[:, pl.ds(W, 64)] = pltpu.roll(tail, 64, 1)[:, :64]
     put(BS, out_skip)
     for j in range(20):
@@ -625,7 +666,7 @@
     scratch = [
         buf((FR, RW, CI, W)),
         buf((6, 4, CI, W)), buf((6, 4, CI, W)), buf((SC * TM, RW, CO, W)), buf((6, 4, CO, W)),
-        buf((6, 3 * CO, 4 * W)), buf((6, 4, CO, W)), buf((FR, 3 * CO, RW * W)),
+        buf((6, 3 * CO, 4 * W)), buf((6, 4, CO, W)), buf((FR, 3 * CO, RW * W)), buf((2, RW, 3 * CO, 2 * W), F32),
         buf((FR, RW, CO, W)), buf((FR, RW, CO, W)),
         buf((3, 3, 3, CO, CI)), buf((3, 3, 3, CO, CO)), buf((27, CI, CO)), buf((27, CO, CO)),
     ]

time: 84.4 us -> 83.4 us (0.988)
  Pallas kernels: 83.6 us -> 82.6 us
    pallas_call x1, Pallas kernels: 79.9 us -> 78.9 us  [shards(): pl.pallas_call(body, out_shape=(jax.ShapeDtypeStruct(inputs.shape, BF16),...]
where the time goes in v3:
time: 83.4 us; the launch traced here: 83.2 us
  Pallas kernels  82.6 us (99%)
    pallas_call x1, Pallas kernels, shards(): pl.pallas_call(body, out_shape=(jax.ShapeDtypeStruct(inputs.shape, BF16),...  78.9 us
    pallas_call x1, Pallas kernels, shards(): pl.pallas_call(last, out_shape=(jax.ShapeDtypeStruct(inputs.shape, BF16),...  3.7 us

profile of v3, /device:TPU:1, one launch (start us, length us, event | category | flops | bytes accessed | tf_op | source)
XLA Modules:
  0.0 83.2 jit_solution(12596756643889096282)
XLA Ops:
  0.6 78.9 %block_backward.1 = (bf16[1,4,2,192,128]{4,3,2,1,0:T(8,128)(2,1)}, bf16[4096,128]{1,0:T(8,128)(2,1)}, bf16[2048,128]{1,0:T(8,128)(2,1)}) custom-call(s32[1,16]{1,0:T(1,128)} %refs_0_.1, bf16[1,4,2,192,128]{4,3,2,1,0:T(8,128)(2,1)} %refs_1_.1, f32[1,192]{1,0:T(1,128)} %bitcast.3, bf16[3,3,3,96,192]{4,3,2,1,0:T(8,128)(2,1)} %refs_3_.1, f32[1,96]{1,0:T(1,128)} %bitcast.4, ...), custom_call_target="tpu_custom_call" | custom-call | tf_op jit(solution)/shard_map/block_backward/pallas_call | solution.py:688
  79.5 3.7 %assemble.1 = (bf16[1,4,2,192,128]{4,3,2,1,0:T(8,128)(2,1)}, f32[3,3,3,96,192]{4,3,2,1,0:T(8,128)}, f32[2592,96]{1,0:T(8,128)}, f32[96,192]{1,0:T(8,128)}) custom-call(bf16[1,4,2,192,128]{4,3,2,1,0:T(8,128)(2,1)} %get-tuple-element.11.refs_0_, bf16[4096,128]{1,0:T(8,128)(2,1)} %get-tuple-element.12.refs_1_, bf16[2048,128]{1,0:T(8,128)(2,1)} %get-tuple-element.13.refs_2_), custom_call_target="tpu_custom_call" | custom-call | tf_op jit(solution)/shard_map/assemble/pallas_call | solution.py:707

commit v4 on v3

--- a/solution.py
+++ b/solution.py
@@ -80,7 +80,7 @@
 
 
 N_SEMS = 192
-N_LOCAL = 24
+N_LOCAL = 32
 
 
 def when(cond, fn):
@@ -90,9 +90,10 @@
         pl.when(cond)(fn)
 
 
-def kernel(scale, sf, x_hbm, gain_in, win_hbm, gain_mid, wmid_hbm, wskip, sg_hbm,
+def kernel(scale, sf, x_hbm, gain_in_hbm, win_hbm, gain_mid_hbm, wmid_hbm, wskip_hbm, sg_hbm,
            out_x, out_in, out_mid,
-           OX,           XE, H1, SG, CE, CS, GE, GS, ACC, A1, H2, WIN, WMID, WTI, WTM,
+           OX, gain_in, gain_mid, wskip,
+           XE, H1, SG, CE, CS, GE, GS, ACC, A1, H2, WIN, WMID, WTI, WTM,
            g_in, g_mid, rc_in, rc_mid, s_in, s_mid,
            a1_in, b1_in, a1_mid, b1_mid, p_in, p_mid, a2_in, b2_in, a2_mid, b2_mid,
            c_in, c_mid, z_in, z_mid, fin_in, fin_mid,
@@ -125,7 +126,7 @@
     kept = []
 
     def keep(src, dst):
-        copy = pltpu.make_async_copy(src, dst, local.at[4 + len(kept)])
+        copy = pltpu.make_async_copy(src, dst, local.at[7 + len(kept)])
         copy.start()
         kept.append(copy)
 
@@ -152,6 +153,9 @@
         pltpu.make_async_copy(sg_hbm.at[0], SG.at[pl.ds(SC * t, SC)], local.at[1]),
         pltpu.make_async_copy(win_hbm, WIN, local.at[2]),
         pltpu.make_async_copy(wmid_hbm, WMID, local.at[3]),
+        pltpu.make_async_copy(gain_in_hbm, gain_in, local.at[4]),
+        pltpu.make_async_copy(gain_mid_hbm, gain_mid, local.at[5]),
+        pltpu.make_async_copy(wskip_hbm, wskip, local.at[6]),
     ]
     for item in loc:
         item.start()
@@ -222,6 +226,8 @@
     for item in x_halo[2:]:
         item.start()
 
+    for item in loc[4:]:
+        item.wait()
     g1 = column(gain_in[...], CI)
     g2 = column(gain_mid[...], CO)
 
@@ -294,7 +300,7 @@
 
     lax.fori_loop(0, 2, own_mid, 0)
 
-    for item in x_halo:
+    for item in x_halo[:2]:
         item.got()
 
     def h1_rows(f, _):
@@ -306,9 +312,6 @@
         h1_at(f, 1)
         h1_at(f, 2)
         return 0
-
-    lax.fori_loop(0, 6, h1_rows, 0)
-    lax.fori_loop(0, 2, h1_prior, 0)
 
     def forward(f, _):
         acc = jnp.zeros((3 * CO, 2 * W), F32)
@@ -322,7 +325,14 @@
             H2[f, r] = norm_fwd(a1.astype(F32), g2).astype(BF16)
         return 0
 
-    lax.fori_loop(0, FR, forward, 0)
+    lax.fori_loop(2, 6, h1_rows, 0)
+    lax.fori_loop(2, FR, forward, 0)
+    x_halo[2].got()
+    lax.fori_loop(0, 2, h1_prior, 0)
+    for item in x_halo[3:]:
+        item.got()
+    lax.fori_loop(0, 2, h1_rows, 0)
+    lax.fori_loop(0, 2, forward, 0)
 
     for item in cot_halo:
         item.got()
@@ -593,13 +603,29 @@
         item.wait()
 
 
-def assemble(scale, gx, fi, fm, out_x, out_in, out_mid, out_skip, BI, BM, BS, sem):
+def assemble(scale, gx_hbm, fi_hbm, fm_hbm, out_x, out_in, out_mid, out_skip, gx, fi, fm, BI, BM, BS, sem, got):
     copies = []
 
     def put(src, dst):
         copy = pltpu.make_async_copy(src, dst, sem.at[len(copies)])
         copy.start()
         copies.append(copy)
+
+    def load(src, dst, i):
+        copy = pltpu.make_async_copy(src, dst, got.at[i])
+        copy.start()
+        return copy
+
+    need_in = []
+    for n in range(5):
+        count = 432 if n < 4 else 320
+        need_in.append([load(fi_hbm.at[pl.ds(at, count)], fi.at[pl.ds(at, count)], 2 * n + k)
+                        for k, at in enumerate((432 * n, 2048 + 432 * n))])
+    need_mid = []
+    for n in range(5):
+        part = pl.ds(480 * n, 480 if n < 4 else 128)
+        need_mid.append(load(fm_hbm.at[part], fm.at[part], 10 + n))
+    need_x = load(gx_hbm, gx, 15)
 
     def rows(n, at, count):
         if at + count <= 432:
@@ -611,8 +637,9 @@
             value = jnp.concatenate([fi[pl.ds(432 * n + at, cut)], fi[pl.ds(2048 + 432 * n, count - cut)]], axis=0)
         return value.astype(F32) * scale
 
-    put(gx, out_x)
     for n, taps in enumerate(PAIRS):
+        for item in need_in[n]:
+            item.wait()
         for kw in range(3):
             low = rows(n, 576 + CO * kw, CO)
             for j, i in enumerate(taps):
@@ -622,10 +649,15 @@
                 BI[kt, kh, kw, :, pl.ds(W, 64)] = rest[:, :64]
         for i in taps:
             put(BI.at[TAPS[i]], out_in.at[TAPS[i]])
+    for item in need_in[4]:
+        item.wait()
     for kw in range(3):
         BI[2, 2, kw, :, pl.ds(0, W)] = fi[pl.ds(1728 + CO * kw, CO)].astype(F32) * scale
         BI[2, 2, kw, :, pl.ds(W, 64)] = (fi[pl.ds(3776 + CO * kw, CO)].astype(F32) * scale)[:, :64]
     put(BI.at[2, 2], out_in.at[2, 2])
+    need_x.wait()
+    put(gx, out_x)
+    need_mid[4].wait()
     tail = fm[pl.ds(1920, CO)].astype(F32) * scale
     BS[pl.ds(0, 32), pl.ds(0, W)] = fm[pl.ds(2016, 32)].astype(F32) * scale
     BS[pl.ds(32, 32), pl.ds(0, W)] = fi[pl.ds(2016, 32)].astype(F32) * scale
@@ -633,6 +665,8 @@
     BS[:, pl.ds(W, 64)] = pltpu.roll(tail, 64, 1)[:, :64]
     put(BS, out_skip)
     for j in range(20):
+        if j % 5 == 0:
+            need_mid[j // 5].wait()
         BM[pl.ds(W * j, W)] = (fm[pl.ds(CO * j, CO)].astype(F32) * scale).T
         if j % 5 == 4:
             rows = pl.ds(W * (j - 4), 5 * W)
@@ -655,7 +689,6 @@
 def shards(inputs, gain_in, conv_in, gain_mid, conv_mid, conv_skip, scored_grads, scored_frames):
     count = scored_frames.shape[1] * inputs.shape[0] * lax.axis_size("dp")
     scale = 1.0 / math.sqrt(count * RW * HT * W)
-    vmem = pl.BlockSpec(memory_space=pltpu.VMEM)
     anyw = pl.BlockSpec(memory_space=pl.ANY)
     smem = pl.BlockSpec(memory_space=pltpu.SMEM)
     big, small = reduce_scratch(ROWS_IN), reduce_scratch(ROWS_MID)
@@ -664,7 +697,7 @@
         return pltpu.VMEM(shape, dtype)
 
     scratch = [
-        buf((FR, RW, CI, W)),
+        buf((FR, RW, CI, W)), buf((1, CI), F32), buf((1, CO), F32), buf((CO, CI)),
         buf((6, 4, CI, W)), buf((6, 4, CI, W)), buf((SC * TM, RW, CO, W)), buf((6, 4, CO, W)),
         buf((6, 3 * CO, 4 * W)), buf((6, 4, CO, W)), buf((FR, 3 * CO, RW * W)), buf((2, RW, 3 * CO, 2 * W), F32),
         buf((FR, RW, CO, W)), buf((FR, RW, CO, W)),
@@ -692,7 +725,7 @@
             jax.ShapeDtypeStruct((ROWS_IN, W), BF16),
             jax.ShapeDtypeStruct((ROWS_MID, W), BF16),
         ),
-        in_specs=[smem, anyw, vmem, anyw, vmem, anyw, vmem, anyw],
+        in_specs=[smem] + [anyw] * 7,
         out_specs=(anyw, anyw, anyw),
         scratch_shapes=scratch,
         compiler_params=pltpu.CompilerParams(
@@ -712,11 +745,12 @@
             jax.ShapeDtypeStruct((27 * CO, CO), F32),
             jax.ShapeDtypeStruct(conv_skip.shape, F32),
         ),
-        in_specs=[vmem, vmem, vmem],
+        in_specs=[anyw, anyw, anyw],
         out_specs=(anyw, anyw, anyw, anyw),
         scratch_shapes=[
+            buf(inputs.shape), buf((ROWS_IN, W)), buf((ROWS_MID, W)),
             buf(conv_in.shape, F32), buf((27 * CO, CO), F32), buf(conv_skip.shape, F32),
-            pltpu.SemaphoreType.DMA((16,)),
+            pltpu.SemaphoreType.DMA((16,)), pltpu.SemaphoreType.DMA((16,)),
         ],
         compiler_params=pltpu.CompilerParams(vmem_limit_bytes=63 * 1024 * 1024),
         name="assemble",

time: 83.4 us -> 81.3 us (0.975)
  Pallas kernels: 82.6 us -> 80.5 us
    pallas_call x1, Pallas kernels: 78.9 us -> 77.1 us  [shards(): pl.pallas_call(body, out_shape=(jax.ShapeDtypeStruct(inputs.shape, BF16),...]
where the time goes in v4:
time: 81.3 us; the launch traced here: 81.1 us
  Pallas kernels  80.5 us (99%)
    pallas_call x1, Pallas kernels, shards(): pl.pallas_call(body, out_shape=(jax.ShapeDtypeStruct(inputs.shape, BF16),...  77.1 us
    pallas_call x1, Pallas kernels, shards(): pl.pallas_call(last, out_shape=(jax.ShapeDtypeStruct(inputs.shape, BF16),...  3.42 us

profile of v4, /device:TPU:1, one launch (start us, length us, event | category | flops | bytes accessed | tf_op | source)
XLA Modules:
  0.0 81.1 jit_solution(8093783152980748579)
XLA Ops:
  0.6 77.1 %block_backward.1 = (bf16[1,4,2,192,128]{4,3,2,1,0:T(8,128)(2,1)}, bf16[4096,128]{1,0:T(8,128)(2,1)}, bf16[2048,128]{1,0:T(8,128)(2,1)}) custom-call(s32[1,16]{1,0:T(1,128)} %refs_0_.1, bf16[1,4,2,192,128]{4,3,2,1,0:T(8,128)(2,1)} %refs_1_.1, f32[1,192]{1,0:T(1,128)} %bitcast.3, bf16[3,3,3,96,192]{4,3,2,1,0:T(8,128)(2,1)} %refs_3_.1, f32[1,96]{1,0:T(1,128)} %bitcast.4, ...), custom_call_target="tpu_custom_call" | custom-call | tf_op jit(solution)/shard_map/block_backward/pallas_call | solution.py:721
  77.7 3.4 %assemble.1 = (bf16[1,4,2,192,128]{4,3,2,1,0:T(8,128)(2,1)}, f32[3,3,3,96,192]{4,3,2,1,0:T(8,128)}, f32[2592,96]{1,0:T(8,128)}, f32[96,192]{1,0:T(8,128)}) custom-call(bf16[1,4,2,192,128]{4,3,2,1,0:T(8,128)(2,1)} %get-tuple-element.11.refs_0_, bf16[4096,128]{1,0:T(8,128)(2,1)} %get-tuple-element.12.refs_1_, bf16[2048,128]{1,0:T(8,128)(2,1)} %get-tuple-element.13.refs_2_), custom_call_target="tpu_custom_call" | custom-call | tf_op jit(solution)/shard_map/assemble/pallas_call | solution.py:740

commit v5 on v4

--- a/solution.py
+++ b/solution.py
@@ -199,7 +199,7 @@
 
     other_t = (t + TM // 2) % TM
     across = [Copy(sg_hbm.at[0, j], SG.at[SC * t + j], dev(tt=other_t)) for j in range(SC)]
-    along = [Copy(sg_hbm.at[0], SG.at[pl.ds(SC * t, SC)], y_peer((y + k) % 4)) for k in (1, 3, 2)]
+    along = [Copy(sg_hbm.at[0], SG.at[pl.ds(SC * t, SC)], y_peer((y + k) % 4)) for k in (2, 1, 3)]
     for item in across + along:
         item.start()
 
@@ -219,7 +219,7 @@
     for j in range(SC):
         across[j].got()
         at_j = SC * other_t + j
-        onward = [Copy(SG.at[at_j], SG.at[at_j], y_peer((y + k) % 4)) for k in (1, 3, 2)]
+        onward = [Copy(SG.at[at_j], SG.at[at_j], y_peer((y + k) % 4)) for k in (2, 1, 3)]
         for item in onward:
             item.start()
         along += onward
@@ -239,22 +239,11 @@
 
     def turn(i, _):
         kt, kh, kw = i // 9, (i // 3) % 3, i % 3
-        WTI[i] = WIN[kt, kh, kw].astype(F32).T.astype(BF16)
         WTM[i] = WMID[kt, kh, kw].astype(F32).T.astype(BF16)
         return 0
 
     lax.fori_loop(0, 27, turn, 0)
-    loc[0].wait()
-
-    def h1_own(i, _):
-        h1_at(2 + i // 2, 1 + i % 2)
-        return 0
-
-    lax.fori_loop(0, 8, h1_own, 0)
-
-    loc[1].wait()
-    for item in along:
-        item.got()
+    places = []
     for f in range(6):
         frame = t * FR + f
         at = jnp.int32(0)
@@ -263,7 +252,11 @@
             hit = (sf[0, j] == frame).astype(jnp.int32)
             at = jnp.maximum(at, j * hit)
             found = jnp.maximum(found, hit)
-        factor = found.astype(F32)
+        places.append((at, found.astype(F32)))
+    loc[1].wait()
+    for item in along:
+        item.got()
+    for f, (at, factor) in enumerate(places):
         for r in range(RW):
             CE[f, 1 + r] = (SG[at, r].astype(F32) * factor).astype(BF16)
     cot_halo = [
@@ -272,6 +265,14 @@
     ]
     for item in cot_halo:
         item.start()
+
+    loc[0].wait()
+
+    def h1_own(i, _):
+        h1_at(2 + i // 2, 1 + i % 2)
+        return 0
+
+    lax.fori_loop(0, 8, h1_own, 0)
 
     skip_a = jnp.zeros((CO, W), F32)
     skip_b = jnp.zeros((CO, W), F32)
@@ -587,12 +588,20 @@
             grad = norm_pull(XE[2 + f, 1 + r].astype(F32), g1, gh1) + skip[:, r * W:(r + 1) * W]
             OX[f, r] = grad.astype(BF16)
 
+    def turn_in(i, _):
+        WTI[i] = WIN[i // 9, (i // 3) % 3, i % 3].astype(F32).T.astype(BF16)
+        return 0
+
+    lax.fori_loop(0, 27, turn_in, 0)
+    next(big)
+    next(small)
     for item in ga_halo:
         item.got()
     for f in range(FR):
         back_in(f)
-        next(big)
-        next(small)
+        if f < 3:
+            next(big)
+            next(small)
     keep(OX, out_x.at[0])
     for _ in range(3):
         next(big)

time: 81.3 us -> 80.7 us (level)
  no operation moved by 1% of the time
where the time goes in v5:
time: 80.7 us; the launch traced here: 80.6 us
  Pallas kernels  79.9 us (99%)
    pallas_call x1, Pallas kernels, shards(): pl.pallas_call(body, out_shape=(jax.ShapeDtypeStruct(inputs.shape, BF16),...  76.5 us
    pallas_call x1, Pallas kernels, shards(): pl.pallas_call(last, out_shape=(jax.ShapeDtypeStruct(inputs.shape, BF16),...  3.42 us

profile of v5, /device:TPU:1, one launch (start us, length us, event | category | flops | bytes accessed | tf_op | source)
XLA Modules:
  0.0 80.6 jit_solution(8305690851157700812)
XLA Ops:
  0.6 76.5 %block_backward.1 = (bf16[1,4,2,192,128]{4,3,2,1,0:T(8,128)(2,1)}, bf16[4096,128]{1,0:T(8,128)(2,1)}, bf16[2048,128]{1,0:T(8,128)(2,1)}) custom-call(s32[1,16]{1,0:T(1,128)} %refs_0_.1, bf16[1,4,2,192,128]{4,3,2,1,0:T(8,128)(2,1)} %refs_1_.1, f32[1,192]{1,0:T(1,128)} %bitcast.3, bf16[3,3,3,96,192]{4,3,2,1,0:T(8,128)(2,1)} %refs_3_.1, f32[1,96]{1,0:T(1,128)} %bitcast.4, ...), custom_call_target="tpu_custom_call" | custom-call | tf_op jit(solution)/shard_map/block_backward/pallas_call | solution.py:730
  77.2 3.4 %assemble.1 = (bf16[1,4,2,192,128]{4,3,2,1,0:T(8,128)(2,1)}, f32[3,3,3,96,192]{4,3,2,1,0:T(8,128)}, f32[2592,96]{1,0:T(8,128)}, f32[96,192]{1,0:T(8,128)}) custom-call(bf16[1,4,2,192,128]{4,3,2,1,0:T(8,128)(2,1)} %get-tuple-element.11.refs_0_, bf16[4096,128]{1,0:T(8,128)(2,1)} %get-tuple-element.12.refs_1_, bf16[2048,128]{1,0:T(8,128)(2,1)} %get-tuple-element.13.refs_2_), custom_call_target="tpu_custom_call" | custom-call | tf_op jit(solution)/shard_map/assemble/pallas_call | solution.py:749
